TPU v7x, 32 devices: a whole 2x2x4 slice. The times are simulated.
32 devices in a mesh: seq: 16 (over z, y, x), tp: 2 (over core).
Axes of the slice: x: 2, y: 2, z: 4, core: 2. Of those that a mesh axis runs over, the one named last changes fastest.
Arguments:
- tokens: bfloat16 [4096, 1536], P('seq'), may hold values from -6 to 6
- cotangent: bfloat16 [4096, 1536], P('seq'), may hold values from -6 to 6
- step_embed: bfloat16 [4, 1024], replicated, may hold values from -6 to 6
- item_band: int32 [4], replicated, may hold values from 0 to 3, as said below
- item_length: int32 [4], replicated, may hold values from 512 to 1024, as said below
- item_width: int32 [4], replicated, may hold values from 16 to 64
- text_states: bfloat16 [1024, 4096], P('seq'), may hold values from -6 to 6
- ada_weight: bfloat16 [1024, 6144], P(None, 'tp'), may hold values from -0.1875 to 0.1875
- ada_bias: float32 [6144], P('tp'), may hold values from -1.5 to 1.5
- attn_gain: float32 [1536], replicated, may hold values from 0.5 to 1.5
- ffn_gain: float32 [1536], replicated, may hold values from 0.5 to 1.5
- query_weight: bfloat16 [1536, 1536], P(None, 'tp'), may hold values from -0.15625 to 0.15625
- key_weight: bfloat16 [1536, 1536], P(None, 'tp'), may hold values from -0.15625 to 0.15625
- value_weight: bfloat16 [1536, 1536], P(None, 'tp'), may hold values from -0.15625 to 0.15625
- query_gain: float32 [1536], P('tp'), may hold values from 1 to 2
- key_gain: float32 [1536], P('tp'), may hold values from 1 to 2
- cross_gate: float32 [24], P('tp'), may hold values from 0.3 to 1.2
- text_key_weight: bfloat16 [4096, 1536], P(None, 'tp'), may hold values from -0.09375 to 0.09375
- text_value_weight: bfloat16 [4096, 1536], P(None, 'tp'), may hold values from -0.09375 to 0.09375
- text_key_gain: float32 [1536], P('tp'), may hold values from 1 to 2
- out_weight: bfloat16 [1536, 1536], P('tp'), may hold values from -3.5 to 3.5
- gate_weight: bfloat16 [1536, 4096], P(None, 'tp'), may hold values from -0.15625 to 0.15625
- up_weight: bfloat16 [1536, 4096], P(None, 'tp'), may hold values from -0.15625 to 0.15625
- down_weight: bfloat16 [4096, 1536], P('tp'), may hold values from -0.09375 to 0.09375
Outputs:
- block_out: bfloat16 [4096, 1536], P('seq')
- tokens_grad: bfloat16 [4096, 1536], P('seq')
- text_grad: float32 [1024, 4096], P('seq', 'tp')
- ada_weight_grad: float32 [1024, 6144], P('seq', 'tp')
- ada_bias_grad: float32 [6144], P('tp')
- attn_gain_grad: float32 [1536], replicated
- ffn_gain_grad: float32 [1536], replicated
- query_weight_grad: float32 [1536, 1536], P('seq', 'tp')
- key_weight_grad: float32 [1536, 1536], P('seq', 'tp')
- value_weight_grad: float32 [1536, 1536], P('seq', 'tp')
- query_gain_grad: float32 [1536], P('tp')
- key_gain_grad: float32 [1536], P('tp')
- cross_gate_grad: float32 [24], P('tp')
- text_key_weight_grad: float32 [4096, 1536], P('seq', 'tp')
- text_value_weight_grad: float32 [4096, 1536], P('seq', 'tp')
- text_key_gain_grad: float32 [1536], P('tp')
- out_weight_grad: float32 [1536, 1536], P('tp', 'seq')
- gate_weight_grad: float32 [1536, 4096], P('seq', 'tp')
- up_weight_grad: float32 [1536, 4096], P('seq', 'tp')
- down_weight_grad: float32 [4096, 1536], P('tp', 'seq')
Inputs may be any that keep to these rules, and one draw needn't show every extreme that they name: `item_band`: every band is used by some item. Item i's real tokens are its first item_length[i] positions; one item fills all 1024 positions and another has exactly 512.
All inputs are finite; a program needn't handle non-finite values.
Results may differ from a plain program's by a relative error of at most 0.024.
Values may be sent and summed in bfloat16 or wider, within the bound.
No kernel may reach another device: no remote copies, remote signals or barrier semaphores. Data moves between devices by JAX's collectives and lax.ppermute only.
A program may use at most 256 MiB of HBM per device.

v0:
```python
import jax
import jax.numpy as jnp
from jax import lax
from jax.sharding import PartitionSpec as P

HDIM = 64
NTXT = 256
BANDS = 4
ITEMS = 4
SLOT = 64


EPSILON = 1e-06
ROPE_BASE = 10000.0
HIGHEST = lax.Precision.HIGHEST
NEG_FILL = -1e30


def rms_inverse(values):
    return lax.rsqrt(jnp.mean(values * values, axis=-1, keepdims=True) + EPSILON)


def rope_angles(row_pos, col_pos, head_dim):
    quarter = head_dim // 4
    frequency = ROPE_BASE ** (-jnp.arange(quarter, dtype=jnp.float32) / quarter)
    angles = jnp.stack([row_pos[..., None] * frequency, col_pos[..., None] * frequency], axis=-2)
    return (jnp.cos(angles), jnp.sin(angles))


def rotate(vectors, cosines, sines):
    shape_all = vectors.shape
    paired = vectors.reshape(shape_all[:-1] + (2, 2, shape_all[-1] // 4))
    former = paired[..., 0, :]
    latter = paired[..., 1, :]
    turned = jnp.stack(
        [former * cosines - latter * sines, former * sines + latter * cosines], axis=-2
    )
    return turned.reshape(shape_all)


def head_norm(raw_vals, gain_vec):
    inverse = rms_inverse(raw_vals)
    unit_vec = raw_vals * inverse
    return (unit_vec * gain_vec, unit_vec, inverse)


def head_norm_back(incoming, unit_vec, inverse, gain_vec):
    grad_unit = incoming * gain_vec
    gain_part = jnp.sum(incoming * unit_vec, axis=tuple(range(incoming.ndim - 2)))
    grad_raw = inverse * (
        grad_unit - unit_vec * jnp.mean(grad_unit * unit_vec, axis=-1, keepdims=True)
    )
    return (grad_raw, gain_part)


def token_norm_back(incoming, normed, inverse, gain_vec, scale_mod):
    lifted = 1.0 + scale_mod
    gain_part = jnp.sum(incoming * normed * lifted, axis=(0, 1))
    scale_part = jnp.sum(incoming * normed * gain_vec, axis=1)
    grad_normed = incoming * gain_vec * lifted
    grad_in = inverse * (
        grad_normed - normed * jnp.mean(grad_normed * normed, axis=-1, keepdims=True)
    )
    return (grad_in, gain_part, scale_part)


def attend(query_h, key_h, value_h, key_valid):
    scaling = query_h.shape[-1] ** (-0.5)
    scores = (
        jnp.einsum("isd,ikd->isk", query_h, key_h, preferred_element_type=jnp.float32) * scaling
    )
    if key_valid is not None:
        scores = jnp.where(key_valid[:, None, :], scores, NEG_FILL)
    row_max = jnp.max(scores, axis=-1, keepdims=True)
    exp_scores = jnp.exp(scores - row_max)
    row_total = jnp.sum(exp_scores, axis=-1, keepdims=True)
    probability = (exp_scores / row_total).astype(jnp.bfloat16)
    output = jnp.einsum("isk,ikd->isd", probability, value_h, preferred_element_type=jnp.float32)
    return (output, (row_max + jnp.log(row_total))[..., 0])


def attend_back(query_h, key_h, value_h, key_valid, lse_h, dout_h):
    scaling = query_h.shape[-1] ** (-0.5)
    scores = (
        jnp.einsum("isd,ikd->isk", query_h, key_h, preferred_element_type=jnp.float32) * scaling
    )
    if key_valid is not None:
        scores = jnp.where(key_valid[:, None, :], scores, NEG_FILL)
    probability = jnp.exp(scores - lse_h[..., None])
    d_prob = jnp.einsum("isd,ikd->isk", dout_h, value_h, preferred_element_type=jnp.float32)
    delta_row = jnp.sum(d_prob * probability, axis=-1)
    d_score = (probability * (d_prob - delta_row[..., None])).astype(jnp.bfloat16)
    d_query = (
        jnp.einsum("isk,ikd->isd", d_score, key_h, preferred_element_type=jnp.float32) * scaling
    )
    d_key = (
        jnp.einsum("isk,isd->ikd", d_score, query_h, preferred_element_type=jnp.float32) * scaling
    )
    d_value = jnp.einsum(
        "isk,isd->ikd", probability.astype(jnp.bfloat16), dout_h, preferred_element_type=jnp.float32
    )
    return (d_query, delta_row, d_key, d_value)


def head_total(partial_value):
    return lax.psum(partial_value.astype(jnp.bfloat16), "tp").astype(jnp.float32)


def feature_total(partial_value):
    return lax.psum(partial_value.astype(jnp.bfloat16), "tp").astype(jnp.float32)


def shards(
    tokens,
    cotangent,
    step_embed,
    item_band,
    item_length,
    item_width,
    text_states,
    ada_weight,
    ada_bias,
    attn_gain,
    ffn_gain,
    query_weight,
    key_weight,
    value_weight,
    query_gain,
    key_gain,
    cross_gate,
    text_key_weight,
    text_value_weight,
    text_key_gain,
    out_weight,
    gate_weight,
    up_weight,
    down_weight,
):
    seq_count = lax.axis_size("seq")
    seq_index = lax.axis_index("seq")
    tp_index = lax.axis_index("tp")
    tok_dev, model_width = tokens.shape
    local_width = query_weight.shape[1]
    local_heads = local_width // HDIM
    capacity = SLOT * seq_count
    text_rows = text_states.shape[0]
    mod_cols = ada_weight.shape[1]
    head_shape = (ITEMS, SLOT, local_heads, HDIM)
    silu_embed = jax.nn.silu(step_embed.astype(jnp.float32))
    local_mod = jnp.dot(silu_embed, ada_weight.astype(jnp.float32), precision=HIGHEST) + ada_bias
    band_mod = lax.all_gather(local_mod, "tp", axis=1, tiled=True)
    band_onehot = (item_band[:, None] == jnp.arange(BANDS, dtype=jnp.int32)[None, :]).astype(
        jnp.float32
    )
    item_mod = jnp.dot(band_onehot, band_mod, precision=HIGHEST)
    scale_attn = item_mod[:, None, 0:model_width]
    gate_attn = jnp.tanh(item_mod[:, None, model_width : 2 * model_width])
    scale_ffn = item_mod[:, None, 2 * model_width : 3 * model_width]
    gate_ffn = jnp.tanh(item_mod[:, None, 3 * model_width :])
    slot_pos = seq_index * SLOT + jnp.arange(SLOT, dtype=jnp.int32)
    row_pos = (slot_pos[None, :] // item_width[:, None]).astype(jnp.float32)
    col_pos = (slot_pos[None, :] % item_width[:, None]).astype(jnp.float32)
    cosines, sines = rope_angles(row_pos, col_pos, HDIM)
    cosines = cosines[:, :, None]
    sines = sines[:, :, None]
    key_valid = jnp.arange(capacity, dtype=jnp.int32)[None, :] < item_length[:, None]

    def by_heads(array_in, row_count):
        return jnp.moveaxis(array_in.reshape(ITEMS, row_count, local_heads, HDIM), 2, 0)

    text_key_raw = jnp.dot(
        text_states, text_key_weight, preferred_element_type=jnp.float32
    ).reshape(text_rows, local_heads, HDIM)
    text_gain_vec = text_key_gain.reshape(local_heads, HDIM)
    text_key_normed, text_unit, text_inverse = head_norm(text_key_raw, text_gain_vec)
    text_key_low = text_key_normed.reshape(text_rows, local_width).astype(jnp.bfloat16)
    text_value_low = jnp.dot(
        text_states, text_value_weight, preferred_element_type=jnp.float32
    ).astype(jnp.bfloat16)
    text_key_all, text_value_all = (
        lax.all_gather(text_key_low, "seq", axis=0, tiled=True),
        lax.all_gather(text_value_low, "seq", axis=0, tiled=True),
    )
    residual = tokens.astype(jnp.float32).reshape(ITEMS, SLOT, model_width)
    inverse_one = rms_inverse(residual)
    normed_one = residual * inverse_one
    attn_in = (
        (normed_one * attn_gain * (1.0 + scale_attn))
        .astype(jnp.bfloat16)
        .reshape(tok_dev, model_width)
    )
    query_raw = jnp.dot(attn_in, query_weight, preferred_element_type=jnp.float32).reshape(
        head_shape
    )
    key_raw = jnp.dot(attn_in, key_weight, preferred_element_type=jnp.float32).reshape(head_shape)
    value_low = (
        jnp.dot(attn_in, value_weight, preferred_element_type=jnp.float32)
        .astype(jnp.bfloat16)
        .reshape(ITEMS, SLOT, local_width)
    )
    query_gain_vec = query_gain.reshape(local_heads, HDIM)
    key_gain_vec = key_gain.reshape(local_heads, HDIM)
    query_normed, query_unit, query_inverse = head_norm(query_raw, query_gain_vec)
    key_normed, key_unit, key_inverse = head_norm(key_raw, key_gain_vec)
    query_low = rotate(query_normed, cosines, sines).astype(jnp.bfloat16)
    key_low = (
        rotate(key_normed, cosines, sines).astype(jnp.bfloat16).reshape(ITEMS, SLOT, local_width)
    )
    key_all, value_all = (
        lax.all_gather(key_low, "seq", axis=1, tiled=True),
        lax.all_gather(value_low, "seq", axis=1, tiled=True),
    )
    query_heads = jnp.moveaxis(query_low, 2, 0)
    key_heads = by_heads(key_all, capacity)
    value_heads = by_heads(value_all, capacity)
    text_key_heads = by_heads(text_key_all, NTXT)
    text_value_heads = by_heads(text_value_all, NTXT)

    def forward_head(operands):
        query_h, key_h, value_h, tkey_h, tvalue_h = operands
        self_part, self_stat = attend(query_h, key_h, value_h, key_valid)
        cross_part, cross_stat = attend(query_h, tkey_h, tvalue_h, None)
        return (self_part, self_stat, cross_part, cross_stat)

    self_out, self_lse, cross_out, cross_lse = lax.map(
        forward_head, (query_heads, key_heads, value_heads, text_key_heads, text_value_heads)
    )
    cross_tanh = jnp.tanh(cross_gate)
    combined = self_out + cross_tanh[:, None, None, None] * cross_out
    combined_low = jnp.moveaxis(combined, 0, 2).reshape(tok_dev, local_width).astype(jnp.bfloat16)
    attn_branch = head_total(
        jnp.dot(combined_low, out_weight, preferred_element_type=jnp.float32)
    ).reshape(ITEMS, SLOT, model_width)
    middle = residual + gate_attn * attn_branch
    inverse_two = rms_inverse(middle)
    normed_two = middle * inverse_two
    ffn_in = (
        (normed_two * ffn_gain * (1.0 + scale_ffn))
        .astype(jnp.bfloat16)
        .reshape(tok_dev, model_width)
    )
    gate_pre = jnp.dot(ffn_in, gate_weight, preferred_element_type=jnp.float32)
    up_pre = jnp.dot(ffn_in, up_weight, preferred_element_type=jnp.float32)
    gate_sig = jax.nn.sigmoid(gate_pre)
    hidden = (gate_pre * gate_sig * up_pre).astype(jnp.bfloat16)
    ffn_branch = head_total(
        jnp.dot(hidden, down_weight, preferred_element_type=jnp.float32)
    ).reshape(ITEMS, SLOT, model_width)
    layer_sum = middle + gate_ffn * ffn_branch
    block_out = layer_sum.reshape(tok_dev, model_width).astype(jnp.bfloat16)
    incoming = cotangent.astype(jnp.float32).reshape(ITEMS, SLOT, model_width)
    gate_ffn_tok = incoming * ffn_branch
    d_ffn = (gate_ffn * incoming).reshape(tok_dev, model_width).astype(jnp.bfloat16)
    down_grad = jnp.dot(hidden.T, d_ffn, preferred_element_type=jnp.float32)
    d_hidden = jnp.dot(d_ffn, down_weight.T, preferred_element_type=jnp.float32)
    d_gate_pre = (d_hidden * up_pre * gate_sig * (1.0 + gate_pre * (1.0 - gate_sig))).astype(
        jnp.bfloat16
    )
    d_up_pre = (d_hidden * gate_pre * gate_sig).astype(jnp.bfloat16)
    gate_grad = jnp.dot(ffn_in.T, d_gate_pre, preferred_element_type=jnp.float32)
    up_grad = jnp.dot(ffn_in.T, d_up_pre, preferred_element_type=jnp.float32)
    d_ffn_in = feature_total(
        jnp.dot(d_gate_pre, gate_weight.T, preferred_element_type=jnp.float32)
        + jnp.dot(d_up_pre, up_weight.T, preferred_element_type=jnp.float32)
    )
    d_middle_norm, ffn_gain_part, scale_ffn_part = token_norm_back(
        d_ffn_in.reshape(ITEMS, SLOT, model_width), normed_two, inverse_two, ffn_gain, scale_ffn
    )
    d_middle = incoming + d_middle_norm
    gate_attn_tok = d_middle * attn_branch
    d_attn = (gate_attn * d_middle).reshape(tok_dev, model_width).astype(jnp.bfloat16)
    out_grad = jnp.dot(combined_low.T, d_attn, preferred_element_type=jnp.float32)
    d_combined = jnp.moveaxis(
        jnp.dot(d_attn, out_weight.T, preferred_element_type=jnp.float32).reshape(head_shape), 2, 0
    )
    cross_gate_part = jnp.sum(d_combined * cross_out, axis=(1, 2, 3)) * (
        1.0 - cross_tanh * cross_tanh
    )
    d_self = d_combined.astype(jnp.bfloat16)
    d_cross = (d_combined * cross_tanh[:, None, None, None]).astype(jnp.bfloat16)

    def cross_head(operands):
        query_h, tkey_h, tvalue_h, lse_h, dout_h = operands
        d_query, unused_delta, d_key, d_value = attend_back(
            query_h, tkey_h, tvalue_h, None, lse_h, dout_h
        )
        return (d_query, d_key, d_value)

    d_query_cross, d_text_key_heads, d_text_value_heads = lax.map(
        cross_head, (query_heads, text_key_heads, text_value_heads, cross_lse, d_cross)
    )

    def full_head(operands):
        query_h, key_h, value_h, lse_h, dout_h = operands
        d_query, unused_delta, d_key, d_value = attend_back(
            query_h, key_h, value_h, key_valid, lse_h, dout_h
        )
        return (d_query, d_key, d_value)

    d_query_self, d_key_heads, d_value_heads = lax.map(
        full_head, (query_heads, key_heads, value_heads, self_lse, d_self)
    )
    d_key_own, d_value_own = (
        lax.psum_scatter(
            jnp.moveaxis(d_key_heads, 0, 2)
            .reshape(ITEMS, capacity, local_width)
            .astype(jnp.bfloat16),
            "seq",
            scatter_dimension=1,
            tiled=True,
        ).astype(jnp.float32),
        lax.psum_scatter(
            jnp.moveaxis(d_value_heads, 0, 2)
            .reshape(ITEMS, capacity, local_width)
            .astype(jnp.bfloat16),
            "seq",
            scatter_dimension=1,
            tiled=True,
        ).astype(jnp.float32),
    )
    d_key_rot = d_key_own.reshape(head_shape)
    d_query_rot = jnp.moveaxis(d_query_self + d_query_cross, 0, 2)
    d_query_raw, query_gain_part = head_norm_back(
        rotate(d_query_rot, cosines, -sines), query_unit, query_inverse, query_gain_vec
    )
    d_key_raw, key_gain_part = head_norm_back(
        rotate(d_key_rot, cosines, -sines), key_unit, key_inverse, key_gain_vec
    )
    d_query_low = d_query_raw.reshape(tok_dev, local_width).astype(jnp.bfloat16)
    d_key_low = d_key_raw.reshape(tok_dev, local_width).astype(jnp.bfloat16)
    d_value_low = d_value_own.reshape(tok_dev, local_width).astype(jnp.bfloat16)
    query_grad = jnp.dot(attn_in.T, d_query_low, preferred_element_type=jnp.float32)
    key_grad = jnp.dot(attn_in.T, d_key_low, preferred_element_type=jnp.float32)
    value_grad = jnp.dot(attn_in.T, d_value_low, preferred_element_type=jnp.float32)
    d_attn_in = feature_total(
        jnp.dot(d_query_low, query_weight.T, preferred_element_type=jnp.float32)
        + jnp.dot(d_key_low, key_weight.T, preferred_element_type=jnp.float32)
        + jnp.dot(d_value_low, value_weight.T, preferred_element_type=jnp.float32)
    )
    d_input_norm, attn_gain_part, scale_attn_part = token_norm_back(
        d_attn_in.reshape(ITEMS, SLOT, model_width), normed_one, inverse_one, attn_gain, scale_attn
    )
    tokens_grad = (d_middle + d_input_norm).reshape(tok_dev, model_width).astype(jnp.bfloat16)
    d_text_key_own, d_text_value_own = (
        lax.psum_scatter(
            jnp.moveaxis(d_text_key_heads, 0, 2)
            .reshape(ITEMS * NTXT, local_width)
            .astype(jnp.bfloat16),
            "seq",
            scatter_dimension=0,
            tiled=True,
        ).astype(jnp.float32),
        lax.psum_scatter(
            jnp.moveaxis(d_text_value_heads, 0, 2)
            .reshape(ITEMS * NTXT, local_width)
            .astype(jnp.bfloat16),
            "seq",
            scatter_dimension=0,
            tiled=True,
        ).astype(jnp.float32),
    )
    d_text_key_raw, text_gain_part = head_norm_back(
        d_text_key_own.reshape(text_rows, local_heads, HDIM), text_unit, text_inverse, text_gain_vec
    )
    d_text_key_low = d_text_key_raw.reshape(text_rows, local_width).astype(jnp.bfloat16)
    d_text_value_low = d_text_value_own.astype(jnp.bfloat16)
    text_key_grad = jnp.dot(text_states.T, d_text_key_low, preferred_element_type=jnp.float32)
    text_value_grad = jnp.dot(text_states.T, d_text_value_low, preferred_element_type=jnp.float32)
    text_grad = lax.psum_scatter(
        (
            jnp.dot(d_text_key_low, text_key_weight.T, preferred_element_type=jnp.float32)
            + jnp.dot(d_text_value_low, text_value_weight.T, preferred_element_type=jnp.float32)
        ).astype(jnp.bfloat16),
        "tp",
        scatter_dimension=1,
        tiled=True,
    ).astype(jnp.float32)
    gate_attn_item = jnp.sum(gate_attn_tok, axis=1) * (1.0 - gate_attn[:, 0] * gate_attn[:, 0])
    gate_ffn_item = jnp.sum(gate_ffn_tok, axis=1) * (1.0 - gate_ffn[:, 0] * gate_ffn[:, 0])
    item_grad = jnp.concatenate(
        [scale_attn_part, gate_attn_item, scale_ffn_part, gate_ffn_item], axis=1
    )
    band_grad = jnp.dot(band_onehot.T, item_grad, precision=HIGHEST)
    local_band_grad = lax.dynamic_slice_in_dim(band_grad, tp_index * mod_cols, mod_cols, 1)
    ada_grad = jnp.dot(silu_embed.T, local_band_grad, precision=HIGHEST)
    ada_bias_part = jnp.sum(local_band_grad, axis=0)
    summed = (
        lax.psum_scatter(
            query_grad.astype(jnp.bfloat16), "seq", scatter_dimension=0, tiled=True
        ).astype(jnp.float32),
        lax.psum_scatter(
            key_grad.astype(jnp.bfloat16), "seq", scatter_dimension=0, tiled=True
        ).astype(jnp.float32),
        lax.psum_scatter(
            value_grad.astype(jnp.bfloat16), "seq", scatter_dimension=0, tiled=True
        ).astype(jnp.float32),
        lax.psum_scatter(
            gate_grad.astype(jnp.bfloat16), "seq", scatter_dimension=0, tiled=True
        ).astype(jnp.float32),
        lax.psum_scatter(
            up_grad.astype(jnp.bfloat16), "seq", scatter_dimension=0, tiled=True
        ).astype(jnp.float32),
        lax.psum_scatter(
            text_key_grad.astype(jnp.bfloat16), "seq", scatter_dimension=0, tiled=True
        ).astype(jnp.float32),
        lax.psum_scatter(
            text_value_grad.astype(jnp.bfloat16), "seq", scatter_dimension=0, tiled=True
        ).astype(jnp.float32),
        lax.psum_scatter(
            ada_grad.astype(jnp.bfloat16), "seq", scatter_dimension=0, tiled=True
        ).astype(jnp.float32),
        lax.psum_scatter(
            out_grad.astype(jnp.bfloat16), "seq", scatter_dimension=1, tiled=True
        ).astype(jnp.float32),
        lax.psum_scatter(
            down_grad.astype(jnp.bfloat16), "seq", scatter_dimension=1, tiled=True
        ).astype(jnp.float32),
    )
    smalls = lax.psum(
        (
            attn_gain_part,
            ffn_gain_part,
            query_gain_part.reshape(local_width),
            key_gain_part.reshape(local_width),
            text_gain_part.reshape(local_width),
            cross_gate_part,
            ada_bias_part,
        ),
        "seq",
    )
    return (
        block_out,
        tokens_grad,
        text_grad,
        summed[7],
        smalls[6],
        smalls[0],
        smalls[1],
        summed[0],
        summed[1],
        summed[2],
        smalls[2],
        smalls[3],
        smalls[5],
        summed[5],
        summed[6],
        smalls[4],
        summed[8],
        summed[3],
        summed[4],
        summed[9],
    )


def solution(mesh):
    placed = (
        P("seq", None),
        P("seq", None),
        P(),
        P(),
        P(),
        P(),
        P("seq", None),
        P(None, "tp"),
        P("tp"),
        P(),
        P(),
        P(None, "tp"),
        P(None, "tp"),
        P(None, "tp"),
        P("tp"),
        P("tp"),
        P("tp"),
        P(None, "tp"),
        P(None, "tp"),
        P("tp"),
        P("tp", None),
        P(None, "tp"),
        P(None, "tp"),
        P("tp", None),
    )
    return jax.shard_map(
        shards,
        mesh=mesh,
        in_specs=placed,
        out_specs=(
            P("seq", None),
            P("seq", None),
            P("seq", "tp"),
            P("seq", "tp"),
            P("tp"),
            P(),
            P(),
            P("seq", "tp"),
            P("seq", "tp"),
            P("seq", "tp"),
            P("tp"),
            P("tp"),
            P("tp"),
            P("seq", "tp"),
            P("seq", "tp"),
            P("tp"),
            P("tp", "seq"),
            P("seq", "tp"),
            P("seq", "tp"),
            P("tp", "seq"),
        ),
        check_vma=False,
    )
```

profile of v0, /device:TPU:0, one launch (start us, length us, event | category | flops | bytes accessed | tf_op | source)
XLA Modules:
  0.0 2756.5 jit_solution(9041393991392076212)
XLA Ops:
  57.8 15.1 all-gather.11.cloned.1.call-done
  82.3 50.6 %all-gather.9.cloned.1.call-done = bf16[1024,768]{1,0:T(8,128)(2,1)} async-done(((bf16[64,768]{1,0:T(8,128)(2,1)}), bf16[1024,768]{1,0:T(8,128)(2,1)}) %all-gather.9.cloned.1.call-update) | async-done | bytes 1572880 | tf_op jit(solution)/shard_map/all_gather | solution.py:181
  142.2 87.0 %all-gather.7.cloned.1.call-done = bf16[4,1024,768]{2,0,1:T(4,128)(2,1)} async-done(((bf16[4,64,768]{2,0,1:T(4,128)(2,1)}), bf16[4,1024,768]{2,0,1:T(4,128)(2,1)}) %all-gather.7.cloned.1.call-update) | async-done | bytes 6291472 | tf_op jit(solution)/shard_map/all_gather | solution.py:211
  246.6 78.2 %all-gather.5.cloned.1.call-done = bf16[4,1024,768]{2,0,1:T(4,128)(2,1)} async-done(((bf16[4,64,768]{2,0,1:T(4,128)(2,1)}), bf16[4,1024,768]{2,0,1:T(4,128)(2,1)}) %all-gather.5.cloned.1.call-update) | async-done | bytes 6291472 | tf_op jit(solution)/shard_map/all_gather | solution.py:210
  342.3 93.2 %while.47 = (s32[]{:T(128)}, f32[12,4,64,64]{3,2,0,1:T(8,128)}, f32[12,4,64]{2,1,0:T(4,128)}, f32[12,4,64,64]{3,2,0,1:T(8,128)}, f32[12,4,64]{2,1,0:T(4,128)}, /...) while((s32[]{:T(128)}, f32[12,4,64,64]{3,2,0,1:T(8,128)}, ...), condition=%wide.region_9.10_spmd.clone, body=%wide.region_4.9_spmd.clone.sunk | while | flops 86445568 | bytes 5666961 | solution.py:225
  444.7 17.4 all-reduce.10.cloned.1.call-done
  485.1 20.1 all-reduce.12.cloned.1.call-done
  514.6 119.5 %while.48 = (s32[]{:T(128)}, f32[12,4,64,64]{2,3,0,1:T(8,128)}, bf16[12,4,1024,64]{2,3,0,1:T(8,128)(2,1)}, bf16[12,4,1024,64]{2,3,0,1:T(8,128)(2,1)}, bf16[12,4,...) while((s32[]{:T(128)}, f32[12,4,64,64]{2,3,0,1:T(8,128)}, ...), condition=%wide.region_17.18_spmd.clone, body=%wide.region_15.17_spmd.clone.sunk | while | flops 170413824 | bytes 12207249 | solution.py:300
  655.8 93.6 %while.46 = (s32[]{:T(128)}, f32[12,4,64,64]{2,3,0,1:T(8,128)S(1)}, bf16[12,4,256,64]{2,3,1,0:T(8,128)(2,1)}, bf16[12,4,256,64]{2,3,1,0:T(8,128)(2,1)}, bf16[12,...) while((s32[]{:T(128)}, f32[12,4,64,64]{2,3,0,1:T(8,128)S(1)}, ...), condition=%wide.region_20.21_spmd, body=%wide.region_18.20_spmd.sunk | while | flops 42548992 | bytes 3613817 | solution.py:289
  774.6 241.5 %all-reduce.14.cloned.1.call-done = (bf16[4,1024,768]{2,0,1:T(4,128)(2,1)}, bf16[4,1024,768]{2,0,1:T(4,128)(2,1)}) async-done(((bf16[4,1024,768]{2,0,1:T(4,128)(2,1)}, bf16[4,1024,768]{2,0,1:T(4,128)(2,1)}), (bf16[4,1024,768]{2,0,1:T(4,128)(2,1)}, bf16[4,1024,768]{2,0,1:T(4,128)(2,1)})) %all-reduce.14.cloned.1.call-update) | async-done | bytes 12582928
  1041.6 102.9 %reduce-scatter.16.cloned.1.call-done = bf16[64,768]{1,0:T(8,128)(2,1)} async-done(((bf16[1024,768]{1,0:T(8,128)(2,1)}), bf16[64,768]{1,0:T(8,128)(2,1)}) %reduce-scatter.16.cloned.1.call-update) | async-done | bytes 98320 | tf_op jit(solution)/shard_map/reduce_scatter | solution.py:345
  1151.2 121.7 %reduce-scatter.40.cloned.1.call-done = bf16[64,768]{1,0:T(8,128)(2,1)} async-done(((bf16[1024,768]{1,0:T(8,128)(2,1)}), bf16[64,768]{1,0:T(8,128)(2,1)}) %reduce-scatter.40.cloned.1.call-update) | async-done | bytes 98320
  1327.0 11.9 convolution_convert_fusion.5
  1341.4 100.9 %reduce-scatter.32.cloned.1.call-done = bf16[768,96]{0,1:T(8,128)(2,1)} async-done(((bf16[768,1536]{0,1:T(8,128)(2,1)}), bf16[768,96]{0,1:T(8,128)(2,1)}) %reduce-scatter.32.cloned.1.call-update) | async-done | bytes 147472 | tf_op jit(solution)/shard_map/reduce_scatter | solution.py:412
  1443.9 149.6 %reduce-scatter.38.cloned.1.call-done = bf16[2048,96]{0,1:T(8,128)(2,1)} async-done(((bf16[2048,1536]{0,1:T(8,128)(2,1)}), bf16[2048,96]{0,1:T(8,128)(2,1)}) %reduce-scatter.38.cloned.1.call-update) | async-done | bytes 393232 | tf_op jit(solution)/shard_map/reduce_scatter | solution.py:415
  1595.4 148.9 %reduce-scatter.36.cloned.1.call-done = bf16[96,2048]{1,0:T(8,128)(2,1)} async-done(((bf16[1536,2048]{1,0:T(8,128)(2,1)}), bf16[96,2048]{1,0:T(8,128)(2,1)}) %reduce-scatter.36.cloned.1.call-update) | async-done | bytes 393232 | tf_op jit(solution)/shard_map/reduce_scatter | solution.py:400
  1746.3 148.9 %reduce-scatter.34.cloned.1.call-done = bf16[96,2048]{1,0:T(8,128)(2,1)} async-done(((bf16[1536,2048]{1,0:T(8,128)(2,1)}), bf16[96,2048]{1,0:T(8,128)(2,1)}) %reduce-scatter.34.cloned.1.call-update) | async-done | bytes 393232 | tf_op jit(solution)/shard_map/reduce_scatter | solution.py:397
  1902.1 76.4 %all-reduce.2 = (f32[3072]{0:T(1024)}, f32[1536]{0:T(1024)}, f32[1536]{0:T(1024)}, f32[768]{0:T(1024)}, f32[768]{0:T(1024)}, /*index=5*/f32[12]{0:T(128)}, f32[768]{0:T(1024)}) all-reduce(f32[3072]{0:T(1024)S(1)} %dynamic-slice_reduce_fusion, f32[1536]{0:T(1024)S(1)} %get-tuple-element.538, ...), channel_id=1, replica_groups=mesh['seq'=16,'tp'=2] {'seq'}, use_global_device_ids=true, to_apply=%region_37.38 | all-reduce | flops 8460 | bytes 67680 | tf_op jit(solution)/shard_map/psum | solution.py:419
  1978.5 68.4 %reduce-scatter.30.cloned.1.call-done = bf16[256,768]{0,1:T(8,128)(2,1)} async-done(((bf16[4096,768]{0,1:T(8,128)(2,1)}), bf16[256,768]{0,1:T(8,128)(2,1)}) %reduce-scatter.30.cloned.1.call-update) | async-done | bytes 393232 | tf_op jit(solution)/shard_map/reduce_scatter | solution.py:406
  2049.1 149.1 %reduce-scatter.28.cloned.1.call-done = bf16[256,768]{0,1:T(8,128)(2,1)} async-done(((bf16[4096,768]{0,1:T(8,128)(2,1)}), bf16[256,768]{0,1:T(8,128)(2,1)}) %reduce-scatter.28.cloned.1.call-update) | async-done | bytes 393232 | tf_op jit(solution)/shard_map/reduce_scatter | solution.py:403
  2200.2 131.2 %reduce-scatter.26.cloned.1.call-done = bf16[96,768]{1,0:T(8,128)(2,1)} async-done(((bf16[1536,768]{1,0:T(8,128)(2,1)}), bf16[96,768]{1,0:T(8,128)(2,1)}) %reduce-scatter.26.cloned.1.call-update) | async-done | bytes 147472 | tf_op jit(solution)/shard_map/reduce_scatter | solution.py:394
  2333.0 130.9 %reduce-scatter.24.cloned.1.call-done = bf16[96,768]{1,0:T(8,128)(2,1)} async-done(((bf16[1536,768]{1,0:T(8,128)(2,1)}), bf16[96,768]{1,0:T(8,128)(2,1)}) %reduce-scatter.24.cloned.1.call-update) | async-done | bytes 147472 | tf_op jit(solution)/shard_map/reduce_scatter | solution.py:391
  2465.6 131.6 %reduce-scatter.22.cloned.1.call-done = bf16[96,768]{1,0:T(8,128)(2,1)} async-done(((bf16[1536,768]{1,0:T(8,128)(2,1)}), bf16[96,768]{1,0:T(8,128)(2,1)}) %reduce-scatter.22.cloned.1.call-update) | async-done | bytes 147472 | tf_op jit(solution)/shard_map/reduce_scatter | solution.py:388
  2598.8 148.5 %reduce-scatter.20.cloned.1.call-done = bf16[64,3072]{1,0:T(8,128)(2,1)} async-done(((bf16[1024,3072]{1,0:T(8,128)(2,1)}), bf16[64,3072]{1,0:T(8,128)(2,1)}) %reduce-scatter.20.cloned.1.call-update) | async-done | bytes 393232 | tf_op jit(solution)/shard_map/reduce_scatter | solution.py:409
  (738 shorter events, 608.3 us)
Async XLA Ops:
  7.2 65.7 %all-gather.11.cloned.1.call-start = ((), (), s32[]{:S(2)}) async-start(), calls=%async_computation.16 | async-start | bytes 1671168 | tf_op jit(solution)/shard_map/all_gather | solution.py:182
  12.2 120.7 %all-gather.9.cloned.1.call-start = ((), (), s32[]{:S(2)}) async-start(), calls=%async_computation.15 | async-start | bytes 1671168 | tf_op jit(solution)/shard_map/all_gather | solution.py:181
  19.7 209.5 %all-gather.7.cloned.1.call-start = ((), (), s32[]{:S(2)}) async-start(), calls=%async_computation.14 | async-start | bytes 6684672 | tf_op jit(solution)/shard_map/all_gather | solution.py:211
  32.4 292.5 %all-gather.5.cloned.1.call-start = ((), (), s32[]{:S(2)}) async-start(), calls=%async_computation.13 | async-start | bytes 6684672 | tf_op jit(solution)/shard_map/all_gather | solution.py:210
  53.2 408.8 %all-reduce.10.cloned.1.call-start = ((), (), s32[]{:S(2)}) async-start(), calls=%async_computation.17 | async-start | bytes 1572864 | tf_op jit(solution)/shard_map/psum | solution.py:106
  444.4 60.8 %all-reduce.12.cloned.1.call-start = ((), (), s32[]{:S(2)}) async-start(), calls=%async_computation.18 | async-start | bytes 1572864 | tf_op jit(solution)/shard_map/psum | solution.py:110
  484.7 531.5 %all-reduce.14.cloned.1.call-start = ((), (), s32[]{:S(2)}) async-start(), calls=%async_computation.32 | async-start | bytes 25165824
  655.6 488.9 %reduce-scatter.16.cloned.1.call-start = ((), (), s32[]{:S(2)}) async-start(), calls=%async_computation.19 | async-start | bytes 1671168 | tf_op jit(solution)/shard_map/reduce_scatter | solution.py:345
  757.4 515.5 %reduce-scatter.40.cloned.1.call-start = ((), (), s32[]{:S(2)}) async-start(), calls=%async_computation.31 | async-start | bytes 1671168
  770.3 552.0 %all-reduce.16.cloned.1.call-start = ((), (), s32[]{:S(2)}) async-start(), calls=%async_computation.33 | async-start | bytes 3145728 | tf_op jit(solution)/shard_map/psum | solution.py:106
  1040.9 298.7 %reduce-scatter.18.cloned.1.call-start = ((), (), s32[]{:S(2)}) async-start(), calls=%async_computation.20 | async-start | bytes 786432 | tf_op jit(solution)/shard_map/reduce_scatter | solution.py:369
  1278.6 163.7 %reduce-scatter.32.cloned.1.call-start = ((), (), s32[]{:S(2)}) async-start(), calls=%async_computation.27 | async-start | bytes 2506752 | tf_op jit(solution)/shard_map/reduce_scatter | solution.py:412
  1282.2 311.3 %reduce-scatter.38.cloned.1.call-start = ((), (), s32[]{:S(2)}) async-start(), calls=%async_computation.30 | async-start | bytes 6684672 | tf_op jit(solution)/shard_map/reduce_scatter | solution.py:415
  1289.1 455.2 %reduce-scatter.36.cloned.1.call-start = ((), (), s32[]{:S(2)}) async-start(), calls=%async_computation.29 | async-start | bytes 6684672 | tf_op jit(solution)/shard_map/reduce_scatter | solution.py:400
  1296.0 599.1 %reduce-scatter.34.cloned.1.call-start = ((), (), s32[]{:S(2)}) async-start(), calls=%async_computation.28 | async-start | bytes 6684672 | tf_op jit(solution)/shard_map/reduce_scatter | solution.py:397
  1301.8 745.0 %reduce-scatter.30.cloned.1.call-start = ((), (), s32[]{:S(2)}) async-start(), calls=%async_computation.26 | async-start | bytes 6684672 | tf_op jit(solution)/shard_map/reduce_scatter | solution.py:406
  1307.4 890.7 %reduce-scatter.28.cloned.1.call-start = ((), (), s32[]{:S(2)}) async-start(), calls=%async_computation.25 | async-start | bytes 6684672 | tf_op jit(solution)/shard_map/reduce_scatter | solution.py:403
  1312.0 1019.4 %reduce-scatter.26.cloned.1.call-start = ((), (), s32[]{:S(2)}) async-start(), calls=%async_computation.24 | async-start | bytes 2506752 | tf_op jit(solution)/shard_map/reduce_scatter | solution.py:394
  1315.3 1148.7 %reduce-scatter.24.cloned.1.call-start = ((), (), s32[]{:S(2)}) async-start(), calls=%async_computation.23 | async-start | bytes 2506752 | tf_op jit(solution)/shard_map/reduce_scatter | solution.py:391
  1318.6 1278.6 %reduce-scatter.22.cloned.1.call-start = ((), (), s32[]{:S(2)}) async-start(), calls=%async_computation.22 | async-start | bytes 2506752 | tf_op jit(solution)/shard_map/reduce_scatter | solution.py:388
  1321.8 1425.5 %reduce-scatter.20.cloned.1.call-start = ((), (), s32[]{:S(2)}) async-start(), calls=%async_computation.21 | async-start | bytes 6684672 | tf_op jit(solution)/shard_map/reduce_scatter | solution.py:409
  1443.9 453.2 %copy-start.84 = (f32[12,64]{1,0:T(8,128)S(1)}, f32[12,64]{1,0:T(8,128)}, u32[]{:S(2)}) copy-start(f32[12,64]{1,0:T(8,128)} %get-tuple-element.536) | copy-start | bytes 9220
  1443.9 453.3 %copy-start.63 = (f32[4,1536]{1,0:T(4,128)S(1)}, f32[4,1536]{1,0:T(4,128)}, u32[]{:S(2)}) copy-start(f32[4,1536]{1,0:T(4,128)} %copy-done.62) | copy-start | bytes 73732
  2046.9 702.4 %copy-start.1 = (bf16[768,1536]{1,0:T(8,128)(2,1)S(1)}, bf16[768,1536]{1,0:T(8,128)(2,1)}, u32[]{:S(2)}) copy-start(bf16[768,1536]{1,0:T(8,128)(2,1)} %param.50) | copy-start | bytes 7077892
  (105 other events, 2148.9 us)
Sparse Core Ops, SparseCore 0:
  12.4 60.5 all-gather.10
  76.3 56.5 all-gather.8
  136.3 92.8 all-gather.6
  232.4 92.4 all-gather.4
  444.5 17.4 all-reduce.9
  484.8 20.3 all-reduce.11
  655.7 360.3 all-reduce.13
  1020.9 123.5 reduce-scatter.15
  1149.3 123.5 reduce-scatter.39
  1276.3 19.4 all-reduce.15
  1298.7 9.1 reduce-scatter.17
  1312.6 129.6 reduce-scatter.31
  1448.4 145.0 reduce-scatter.37
  1599.4 144.8 reduce-scatter.35
  1750.2 144.8 reduce-scatter.33
  1901.0 145.7 reduce-scatter.29
  2052.8 145.3 reduce-scatter.27
  2203.7 127.6 reduce-scatter.25
  2336.3 127.6 reduce-scatter.23
  2469.5 127.6 reduce-scatter.21
  2602.4 144.8 reduce-scatter.19
where the time goes:
time: 2770 us; the launch traced here: 2760 us
  waiting for transfers between devices  2040 us (74%)
  matrix products  373 us (13%)
  local copies, waits for them, and re-layouts  168 us (6%)
  blocking collectives  78.5 us (3%)
  other arithmetic  75 us (3%)
    unnamed x23, waiting for transfers between devices  364 us
    reduce_scatter x1, waiting for transfers between devices, shards(): lax.psum_scatter(down_grad.astype(jnp.bfloat16), 'seq', scatter_dimension...  150 us
    reduce_scatter x1, waiting for transfers between devices, shards(): lax.psum_scatter(text_key_grad.astype(jnp.bfloat16), 'seq', scatter_dimen...  149 us
    reduce_scatter x1, waiting for transfers between devices, shards(): lax.psum_scatter(up_grad.astype(jnp.bfloat16), 'seq', scatter_dimension=0...  149 us
    reduce_scatter x1, waiting for transfers between devices, shards(): lax.psum_scatter(gate_grad.astype(jnp.bfloat16), 'seq', scatter_dimension...  149 us
    reduce_scatter x1, waiting for transfers between devices, shards(): lax.psum_scatter(ada_grad.astype(jnp.bfloat16), 'seq', scatter_dimension=...  148 us
    reduce_scatter x1, waiting for transfers between devices, shards(): lax.psum_scatter(query_grad.astype(jnp.bfloat16), 'seq', scatter_dimensio...  132 us
    reduce_scatter x1, waiting for transfers between devices, shards(): lax.psum_scatter(value_grad.astype(jnp.bfloat16), 'seq', scatter_dimensio...  131 us
  transfers between devices with their start and end apart: 21, of which 19 were waited for; matrix products, arithmetic and copies ran while one was open for 11% of the time, Pallas kernels for 0%

commit v1 on v0

--- a/solution.py
+++ b/solution.py
@@ -1,6 +1,9 @@
 import jax
 import jax.numpy as jnp
 from jax import lax
+from jax.experimental import pallas as pl
+from jax.experimental.pallas import tpu as pltpu
+from jax.sharding import Mesh
 from jax.sharding import PartitionSpec as P
 
 HDIM = 64
@@ -452,58 +455,684 @@
     )
 
 
-def solution(mesh):
-    placed = (
-        P("seq", None),
-        P("seq", None),
+MESH_AXES = ("z", "y", "x", "c")
+PLANE = 4
+STRIPS = 4
+CORES = 2
+
+
+def device_pairs(target):
+    pairs = []
+    for strip in range(STRIPS):
+        for place in range(PLANE):
+            for core in range(CORES):
+                aim = target(strip, place, core)
+                pairs.append(
+                    (
+                        (strip * PLANE + place) * CORES + core,
+                        (aim[0] * PLANE + aim[1]) * CORES + aim[2],
+                    )
+                )
+    return pairs
+
+
+FLIP_CORE = device_pairs(lambda strip, place, core: (strip, place, 1 - core))
+FLIP_FIRST = device_pairs(lambda strip, place, core: (strip, place ^ (1 + core), core))
+FLIP_SECOND = device_pairs(lambda strip, place, core: (strip, place ^ (2 - core), core))
+FLIP_PLACE = {
+    mask: device_pairs(lambda strip, place, core, mask=mask: (strip, place ^ mask, core))
+    for mask in (1, 2, 3)
+}
+FLIP_STRIP = {
+    mask: device_pairs(lambda strip, place, core, mask=mask: (strip ^ mask, place, core))
+    for mask in (1, 2, 3)
+}
+
+
+def move(value, pairs):
+    return lax.ppermute(value, MESH_AXES, pairs)
+
+
+def plane_gather(own):
+    own = jnp.concatenate([own, move(own, FLIP_FIRST)])
+    own = jnp.concatenate([own, move(own, FLIP_SECOND)])
+    return jnp.concatenate([own, move(own, FLIP_CORE)])
+
+
+def plane_scatter(whole):
+    for pairs in (FLIP_CORE, FLIP_SECOND, FLIP_FIRST):
+        half = whole.shape[0] // 2
+        arrived = move(whole[half:].astype(jnp.bfloat16), pairs)
+        whole = whole[:half].astype(jnp.float32) + arrived.astype(jnp.float32)
+    return whole
+
+
+def plane_sum(value):
+    for pairs in (FLIP_CORE, FLIP_PLACE[1], FLIP_PLACE[2]):
+        value = value + move(value, pairs)
+    return value
+
+
+def strip_gather(value):
+    return [value] + [move(value, FLIP_STRIP[mask]) for mask in (1, 2, 3)]
+
+
+def pair_sum(four):
+    return (four[0] + four[1]) + (four[2] + four[3])
+
+
+def exchange(blocks, index, table):
+    def pick(mask):
+        return lax.dynamic_index_in_dim(blocks, index ^ mask, 0, keepdims=False)
+
+    return [pick(0)] + [move(pick(mask), table[mask]) for mask in (1, 2, 3)]
+
+
+def absolute(relative, index):
+    odd = (index & 1) == 1
+    high = (index & 2) == 2
+    step = [jnp.where(odd, relative[i ^ 1], relative[i]) for i in range(4)]
+    return [jnp.where(high, step[i ^ 2], step[i]) for i in range(4)]
+
+
+def contract(left, right, left_dim, right_dim):
+    return lax.dot_general(
+        left,
+        right,
+        (((left_dim,), (right_dim,)), ((), ())),
+        preferred_element_type=jnp.float32,
+    )
+
+
+def turn(block, cosine, sine):
+    a, b, c, d = block[0:16], block[16:32], block[32:48], block[48:64]
+    cr, cc = cosine[0:16], cosine[16:32]
+    sr, sc = sine[0:16], sine[16:32]
+    return jnp.concatenate(
+        [a * cr - b * sr, a * sr + b * cr, c * cc - d * sc, c * sc + d * cc], axis=0
+    )
+
+
+def unit_of(raw):
+    inverse = lax.rsqrt(jnp.mean(raw * raw, axis=0, keepdims=True) + EPSILON)
+    return raw * inverse, inverse
+
+
+def unit_back(incoming, unit, inverse, gain):
+    lifted = incoming * gain
+    gain_part = jnp.sum(incoming * unit, axis=1, keepdims=True)
+    raw_part = inverse * (lifted - unit * jnp.mean(lifted * unit, axis=0, keepdims=True))
+    return raw_part, gain_part
+
+
+QBLOCK = 256
+
+
+def attend_kernel(
+    q_ref,
+    k_ref,
+    v_ref,
+    tk_ref,
+    tv_ref,
+    qg_ref,
+    kg_ref,
+    tg_ref,
+    cos_ref,
+    sin_ref,
+    valid_ref,
+    gate_ref,
+    comb_ref,
+    self_ref,
+    cross_ref,
+    qlow_ref,
+    klow_ref,
+    tlow_ref,
+    rinv_ref,
+):
+    cosine, sine, valid = cos_ref[...], sin_ref[...], valid_ref[...]
+    query = turn(unit_of(q_ref[...])[0] * qg_ref[...], cosine, sine).astype(jnp.bfloat16)
+    key = turn(unit_of(k_ref[...])[0] * kg_ref[...], cosine, sine)
+    qlow_ref[...] = query
+    klow_ref[...] = key.astype(jnp.bfloat16)
+    key_rows = key.T.astype(jnp.bfloat16)
+    text_key = unit_of(tk_ref[...])[0] * tg_ref[...]
+    tlow_ref[...] = text_key.astype(jnp.bfloat16)
+    text_rows = text_key.T.astype(jnp.bfloat16)
+    value = v_ref[...].astype(jnp.bfloat16).astype(jnp.float32) * valid
+    lanes = value.shape[1]
+    value_ones = jnp.concatenate(
+        [value, jnp.broadcast_to(valid, (16, lanes))], axis=0
+    ).astype(jnp.bfloat16)
+    tvalue = tv_ref[...]
+    tvalue_ones = jnp.concatenate(
+        [tvalue, jnp.ones((16, tvalue.shape[1]), jnp.float32)], axis=0
+    ).astype(jnp.bfloat16)
+    gate = gate_ref[0:1, 0:1]
+    scaled = (query.astype(jnp.float32) * 0.125).astype(jnp.bfloat16)
+    for start in range(0, lanes, QBLOCK):
+        cols = slice(start, start + QBLOCK)
+        weight = jnp.exp(contract(key_rows, scaled[:, cols], 1, 0)).astype(jnp.bfloat16)
+        total = contract(value_ones, weight, 1, 0)
+        rinv = 1.0 / total[64:65]
+        own = total[:64] * rinv
+        tweight = jnp.exp(contract(text_rows, scaled[:, cols], 1, 0)).astype(jnp.bfloat16)
+        ttotal = contract(tvalue_ones, tweight, 1, 0)
+        trinv = 1.0 / ttotal[64:65]
+        text = ttotal[:64] * trinv
+        self_ref[:, cols] = own
+        cross_ref[:, cols] = text
+        rinv_ref[0:1, cols] = rinv
+        rinv_ref[1:2, cols] = trinv
+        comb_ref[:, cols] = (own + gate * text).astype(jnp.bfloat16)
+
+
+def attend_back_kernel(
+    q_ref,
+    k_ref,
+    v_ref,
+    tk_ref,
+    tv_ref,
+    qg_ref,
+    kg_ref,
+    tg_ref,
+    cos_ref,
+    sin_ref,
+    valid_ref,
+    gate_ref,
+    self_ref,
+    cross_ref,
+    qlow_ref,
+    klow_ref,
+    tlow_ref,
+    rinv_ref,
+    dcomb_ref,
+    dq_ref,
+    dk_ref,
+    dv_ref,
+    dtk_ref,
+    dtv_ref,
+    gains_ref,
+):
+    cosine, sine, valid = cos_ref[...], sin_ref[...], valid_ref[...]
+    lanes = valid.shape[1]
+    gate = gate_ref[0:1, 0:1]
+    dcomb = dcomb_ref[...]
+    cross = cross_ref[...]
+    dself = dcomb.astype(jnp.bfloat16)
+    dcross = (dcomb * gate).astype(jnp.bfloat16)
+    delta = jnp.sum(dself.astype(jnp.float32) * self_ref[...], axis=0, keepdims=True)
+    tdelta = jnp.sum(dcross.astype(jnp.float32) * cross, axis=0, keepdims=True)
+    gate_part = jnp.sum(
+        jnp.sum(dcomb * cross, axis=0, keepdims=True), axis=1, keepdims=True
+    ) * (1.0 - gate * gate)
+    query = qlow_ref[...]
+    scaled = (query.astype(jnp.float32) * 0.125).astype(jnp.bfloat16)
+    key = klow_ref[...].astype(jnp.float32)
+    key_rows = key.T.astype(jnp.bfloat16)
+    key_held = (key * valid * 0.125).astype(jnp.bfloat16)
+    value_rows = v_ref[...].T.astype(jnp.bfloat16)
+    text_key = tlow_ref[...].astype(jnp.float32)
+    text_rows = text_key.T.astype(jnp.bfloat16)
+    text_held = (text_key * 0.125).astype(jnp.bfloat16)
+    tvalue_rows = tv_ref[...].T.astype(jnp.bfloat16)
+    dkey = dvalue = dtkey = dtvalue = 0.0
+    dquery = []
+    for start in range(0, lanes, QBLOCK):
+        cols = slice(start, start + QBLOCK)
+        probs = jnp.exp(contract(key_rows, scaled[:, cols], 1, 0)) * rinv_ref[0:1, cols]
+        dprobs = contract(value_rows, dself[:, cols], 1, 0)
+        dscore = (probs * (dprobs - delta[:, cols])).astype(jnp.bfloat16)
+        dvalue += contract(dself[:, cols], probs.astype(jnp.bfloat16), 1, 1)
+        dkey += contract(scaled[:, cols], dscore, 1, 1)
+        turned = contract(key_held, dscore, 1, 0)
+        tprobs = jnp.exp(contract(text_rows, scaled[:, cols], 1, 0)) * rinv_ref[1:2, cols]
+        dtprobs = contract(tvalue_rows, dcross[:, cols], 1, 0)
+        dtscore = (tprobs * (dtprobs - tdelta[:, cols])).astype(jnp.bfloat16)
+        dtvalue += contract(dcross[:, cols], tprobs.astype(jnp.bfloat16), 1, 1)
+        dtkey += contract(scaled[:, cols], dtscore, 1, 1)
+        dquery.append(turned + contract(text_held, dtscore, 1, 0))
+    dquery = jnp.concatenate(dquery, axis=1)
+    unit, inverse = unit_of(q_ref[...])
+    raw, query_gain = unit_back(turn(dquery, cosine, -sine), unit, inverse, qg_ref[...])
+    dq_ref[...] = raw.astype(jnp.bfloat16)
+    unit, inverse = unit_of(k_ref[...])
+    raw, key_gain = unit_back(turn(dkey * valid, cosine, -sine), unit, inverse, kg_ref[...])
+    dk_ref[...] = raw.astype(jnp.bfloat16)
+    dv_ref[...] = (dvalue * valid).astype(jnp.bfloat16)
+    unit, inverse = unit_of(tk_ref[...])
+    raw, text_gain = unit_back(dtkey, unit, inverse, tg_ref[...])
+    dtk_ref[...] = raw.astype(jnp.bfloat16)
+    dtv_ref[...] = dtvalue.astype(jnp.bfloat16)
+    gains_ref[:, 0:128] = jnp.broadcast_to(query_gain, (64, 128))
+    gains_ref[:, 128:256] = jnp.broadcast_to(key_gain, (64, 128))
+    gains_ref[:, 256:384] = jnp.broadcast_to(text_gain, (64, 128))
+    gains_ref[:, 384:512] = jnp.broadcast_to(gate_part, (64, 128))
+
+
+def head_block(width, offset=0):
+    return pl.BlockSpec((HDIM, width), lambda h: (h + offset, 0))
+
+
+def shared_block(rows, width):
+    return pl.BlockSpec((rows, width), lambda h: (0, 0))
+
+
+def attention_call(heads, lanes, texts, backward):
+    f32, b16 = jnp.float32, jnp.bfloat16
+    specs = [
+        head_block(lanes),
+        head_block(lanes, heads),
+        head_block(lanes, 2 * heads),
+        head_block(texts),
+        head_block(texts, heads),
+        head_block(1),
+        head_block(1),
+        head_block(1),
+        shared_block(32, lanes),
+        shared_block(32, lanes),
+        shared_block(1, lanes),
+        pl.BlockSpec((8, 128), lambda h: (h, 0)),
+    ]
+    wide = heads * HDIM
+    rinv_spec = pl.BlockSpec((8, lanes), lambda h: (h, 0))
+    saved = [head_block(lanes)] * 2 + [head_block(lanes)] * 2 + [head_block(texts), rinv_spec]
+    shape = jax.ShapeDtypeStruct
+    pairs = heads * lanes * (lanes + texts)
+    if not backward:
+        out_specs = [head_block(lanes)] + saved
+        out_shape = [
+            shape((wide, lanes), b16),
+            shape((wide, lanes), f32),
+            shape((wide, lanes), f32),
+            shape((wide, lanes), b16),
+            shape((wide, lanes), b16),
+            shape((wide, texts), b16),
+            shape((heads * 8, lanes), f32),
+        ]
+        body, passes = attend_kernel, 2
+    else:
+        specs = specs + saved + [head_block(lanes)]
+        out_specs = [head_block(lanes)] * 3 + [head_block(texts)] * 2 + [head_block(512)]
+        out_shape = (
+            [shape((wide, lanes), b16)] * 3
+            + [shape((wide, texts), b16)] * 2
+            + [shape((wide, 512), f32)]
+        )
+        body, passes = attend_back_kernel, 5
+    return pl.pallas_call(
+        body,
+        grid=(heads,),
+        in_specs=specs,
+        out_specs=out_specs,
+        out_shape=out_shape,
+        compiler_params=pltpu.CompilerParams(vmem_limit_bytes=48 * 1024 * 1024),
+        cost_estimate=pl.CostEstimate(
+            flops=8 * pairs * HDIM * passes, bytes_accessed=8 * wide * lanes, transcendentals=pairs
+        ),
+    )
+
+
+def split_three(value):
+    high = lax.reduce_precision(value, 8, 7)
+    middle = lax.reduce_precision(value - high, 8, 7)
+    return jnp.concatenate([high, middle, value - high - middle]).astype(jnp.bfloat16)
+
+
+def strip_shards(
+    tokens,
+    cotangent,
+    step_embed,
+    item_band,
+    item_length,
+    item_width,
+    text_states,
+    ada_weight,
+    ada_bias,
+    attn_gain,
+    ffn_gain,
+    query_weight,
+    key_weight,
+    value_weight,
+    query_gain,
+    key_gain,
+    cross_gate,
+    text_key_weight,
+    text_value_weight,
+    text_key_gain,
+    out_weight,
+    gate_weight,
+    up_weight,
+    down_weight,
+):
+    f32, b16 = jnp.float32, jnp.bfloat16
+    strip = lax.axis_index("z")
+    place = lax.axis_index("y") * 2 + lax.axis_index("x")
+    core = lax.axis_index("c")
+    first_core = core == 0
+    width = tokens.shape[1]
+    half = SLOT // CORES
+    own_rows = STRIPS * half
+    lanes = own_rows * PLANE * CORES
+    wide = query_weight.shape[1] // PLANE
+    heads = wide // HDIM
+    hidden_wide = gate_weight.shape[1] // PLANE
+    text_own = text_states.shape[0]
+    texts = text_own * PLANE
+
+    def cols(weight, size):
+        return lax.dynamic_slice_in_dim(weight, place * size, size, 1)
+
+    def rows(weight, size):
+        return lax.dynamic_slice_in_dim(weight, place * size, size, 0)
+
+    def to_items(array_in):
+        parts = lax.dynamic_slice_in_dim(
+            array_in.reshape(ITEMS, SLOT, width), core * half, half, 1
+        )
+        return jnp.concatenate(exchange(parts, strip, FLIP_STRIP))
+
+    def from_items(array_in):
+        parts = array_in.reshape(STRIPS, half, width)
+        arrived = [parts[0]] + [move(parts[m], FLIP_STRIP[m]) for m in (1, 2, 3)]
+        mine = jnp.stack(absolute(arrived, strip))
+        other = move(mine, FLIP_CORE)
+        low = jnp.where(first_core, mine, other)
+        high = jnp.where(first_core, other, mine)
+        return jnp.concatenate([low, high], axis=1).reshape(ITEMS * SLOT, width)
+
+    own_tokens = to_items(tokens)
+    all_tokens = plane_gather(own_tokens)
+
+    silu_embed = jax.nn.silu(step_embed.astype(f32))
+    products = jnp.dot(split_three(silu_embed), ada_weight, preferred_element_type=f32)
+    local_mod = products[0:4] + products[4:8] + products[8:12] + ada_bias
+    other_mod = move(local_mod, FLIP_CORE)
+    low_mod = jnp.where(first_core, local_mod, other_mod)
+    high_mod = jnp.where(first_core, other_mod, local_mod)
+
+    def banded(table, mask):
+        return lax.dynamic_index_in_dim(table, item_band[strip ^ mask], 0, keepdims=False)
+
+    scale_attn_items = [banded(low_mod[:, :width], mask) for mask in range(4)]
+    scale_ffn_items = [banded(high_mod[:, :width], mask) for mask in range(4)]
+    lift_attn = attn_gain * (1.0 + scale_attn_items[0])
+    lift_ffn = ffn_gain * (1.0 + scale_ffn_items[0])
+    gate_attn = jnp.tanh(banded(low_mod[:, width:], 0))
+    gate_ffn = jnp.tanh(banded(high_mod[:, width:], 0))
+
+    text_raw = jnp.stack(
+        [
+            contract(text_key_weight, text_states, 0, 1),
+            contract(text_value_weight, text_states, 0, 1).astype(b16).astype(f32),
+        ]
+    )
+    text_raw = jnp.moveaxis(text_raw.reshape(2, PLANE, wide, text_own), 1, 0)
+    text_raw = jnp.concatenate(exchange(text_raw, place, FLIP_PLACE), axis=2)
+    text_raw = text_raw.reshape(2 * wide, texts)
+
+    lane = jnp.arange(lanes, dtype=jnp.int32)
+    block, inner = lane // own_rows, lane % own_rows
+    flipped = block // PLANE
+    from_core = core ^ flipped
+    mask_first, mask_second = 1 + from_core, 2 - from_core
+    from_place = place ^ ((block & 1) * mask_first) ^ (((block // 2) & 1) * mask_second)
+    from_strip = strip ^ (inner // half)
+    position = (from_strip * PLANE + from_place) * SLOT + from_core * half + inner % half
+    width_here = item_width[strip]
+    grid_row = (position // width_here).astype(f32)
+    grid_col = (position % width_here).astype(f32)
+    quarter = HDIM // 4
+    frequency = ROPE_BASE ** (-jnp.arange(quarter, dtype=f32) / quarter)
+    angles = jnp.concatenate(
+        [frequency[:, None] * grid_row[None, :], frequency[:, None] * grid_col[None, :]]
+    )
+    cosine, sine = jnp.cos(angles), jnp.sin(angles)
+    valid = (position < item_length[strip]).astype(f32)[None, :]
+
+    def column(vector):
+        return lax.dynamic_slice_in_dim(vector, place * wide, wide, 0)[:, None]
+
+    tanh_gate = jnp.tanh(lax.dynamic_slice_in_dim(cross_gate, place * heads, heads, 0))
+    gate_tiles = jnp.broadcast_to(tanh_gate[:, None, None], (heads, 8, 128)).reshape(-1, 128)
+
+    residual_all = all_tokens.astype(f32)
+    attn_in = (residual_all * rms_inverse(residual_all) * lift_attn).astype(b16)
+    qkv_weight = jnp.concatenate(
+        [cols(query_weight, wide), cols(key_weight, wide), cols(value_weight, wide)], axis=1
+    )
+    qkv = contract(qkv_weight, attn_in, 0, 1)
+    common = (
+        qkv,
+        qkv,
+        qkv,
+        text_raw,
+        text_raw,
+        column(query_gain),
+        column(key_gain),
+        column(text_key_gain),
+        cosine,
+        sine,
+        valid,
+        gate_tiles,
+    )
+    combined, *saved = attention_call(heads, lanes, texts, False)(*common)
+    out_rows = rows(out_weight, wide)
+    attn_branch = plane_scatter(contract(combined, out_rows, 0, 0).astype(b16))
+
+    residual = own_tokens.reshape(own_rows, width).astype(f32)
+    middle = residual + gate_attn * attn_branch
+    inverse_two = rms_inverse(middle)
+    normed_two = middle * inverse_two
+    ffn_in = plane_gather((normed_two * lift_ffn).astype(b16))
+    incoming = to_items(cotangent)
+    all_incoming = plane_gather(incoming)
+    incoming = incoming.reshape(own_rows, width).astype(f32)
+    d_ffn = (gate_ffn * all_incoming.astype(f32)).astype(b16)
+    gu_weight = jnp.concatenate(
+        [cols(gate_weight, hidden_wide), cols(up_weight, hidden_wide)], axis=1
+    )
+    down_rows = rows(down_weight, hidden_wide)
+    d_hidden = contract(d_ffn, down_rows, 1, 1)
+    gate_up = jnp.dot(ffn_in, gu_weight, preferred_element_type=f32)
+    gate_pre, up_pre = gate_up[:, :hidden_wide], gate_up[:, hidden_wide:]
+    gate_sig = jax.nn.sigmoid(gate_pre)
+    hidden = (gate_pre * gate_sig * up_pre).astype(b16)
+    d_gate = (d_hidden * up_pre * gate_sig * (1.0 + gate_pre * (1.0 - gate_sig))).astype(b16)
+    d_up = (d_hidden * gate_pre * gate_sig).astype(b16)
+    d_gate_up = jnp.concatenate([d_gate, d_up], axis=1)
+    d_ffn_in = plane_scatter(contract(d_gate_up, gu_weight, 1, 1).astype(b16))
+    d_normed = d_ffn_in * normed_two
+    u_ffn = jnp.sum(d_normed, axis=0)
+    d_middle = incoming + inverse_two * (
+        d_ffn_in * lift_ffn
+        - normed_two * jnp.mean(d_normed * lift_ffn, axis=-1, keepdims=True)
+    )
+    w_attn = jnp.sum(d_middle * attn_branch, axis=0) * (1.0 - gate_attn * gate_attn)
+    d_attn = plane_gather((gate_attn * d_middle).astype(b16))
+
+    ffn_branch = plane_scatter(
+        jnp.dot(hidden, down_rows, preferred_element_type=f32).astype(b16)
+    )
+    w_ffn = jnp.sum(incoming * ffn_branch, axis=0) * (1.0 - gate_ffn * gate_ffn)
+    block_out = from_items((middle + gate_ffn * ffn_branch).astype(b16))
+
+    d_comb = contract(out_rows, d_attn, 1, 1)
+    dq, dk, dv, d_text_key, d_text_value, gains = attention_call(heads, lanes, texts, True)(
+        *common, *saved, d_comb
+    )
+    d_qkv = jnp.concatenate([dq, dk, dv])
+    d_attn_in = plane_scatter(contract(d_qkv, qkv_weight, 0, 1).astype(b16))
+    inverse_one = rms_inverse(residual)
+    normed_one = residual * inverse_one
+    d_normed = d_attn_in * normed_one
+    u_attn = jnp.sum(d_normed, axis=0)
+    tokens_grad = d_middle + inverse_one * (
+        d_attn_in * lift_attn
+        - normed_one * jnp.mean(d_normed * lift_attn, axis=-1, keepdims=True)
+    )
+    tokens_grad = from_items(tokens_grad.astype(b16))
+
+    def spread(grad):
+        own = lax.psum_scatter(grad, "z", scatter_dimension=0, tiled=True)
+        blocks = own.reshape(PLANE, own.shape[0] // PLANE, own.shape[1])
+        return absolute(exchange(blocks, place, FLIP_PLACE), place)
+
+    def sheet(blocks, start, size):
+        return jnp.concatenate([b[:, start : start + size] for b in blocks], axis=1).astype(f32)
+
+    ffn_grads = jnp.concatenate(
+        [
+            contract(ffn_in, d_gate_up, 0, 0).astype(b16),
+            contract(d_ffn, hidden, 0, 0).astype(b16),
+            contract(d_attn, combined, 0, 1).astype(b16),
+        ],
+        axis=1,
+    )
+    ffn_blocks = spread(ffn_grads)
+    attn_blocks = spread(contract(attn_in, d_qkv, 0, 1).astype(b16))
+    gate_grad = sheet(ffn_blocks, 0, hidden_wide)
+    up_grad = sheet(ffn_blocks, hidden_wide, hidden_wide)
+    down_grad = sheet(ffn_blocks, 2 * hidden_wide, hidden_wide).T
+    out_grad = sheet(ffn_blocks, 3 * hidden_wide, wide).T
+    query_grad = sheet(attn_blocks, 0, wide)
+    key_grad = sheet(attn_blocks, wide, wide)
+    value_grad = sheet(attn_blocks, 2 * wide, wide)
+
+    d_text = jnp.stack([d_text_key, d_text_value])
+    back = [d_text[:, :, :text_own]] + [
+        move(d_text[:, :, m * text_own : (m + 1) * text_own], FLIP_PLACE[m]) for m in (1, 2, 3)
+    ]
+    back = jnp.concatenate(absolute(back, place), axis=1)
+    text_part = contract(back[0], text_key_weight, 0, 1) + contract(
+        back[1], text_value_weight, 0, 1
+    )
+    text_half = text_part.shape[1] // CORES
+    text_send = lax.dynamic_slice_in_dim(text_part, (1 - core) * text_half, text_half, 1)
+    text_keep = lax.dynamic_slice_in_dim(text_part, core * text_half, text_half, 1)
+    text_grad = text_keep + move(text_send.astype(b16), FLIP_CORE).astype(f32)
+    states_wide = text_states.shape[1] // STRIPS
+    states = jnp.moveaxis(text_states.reshape(text_own, STRIPS, states_wide), 1, 0)
+    states = jnp.stack(exchange(states, strip, FLIP_STRIP))
+    states = jnp.stack(
+        [states] + [move(states, FLIP_PLACE[m]) for m in (1, 2, 3)], axis=1
+    ).reshape(STRIPS * texts, states_wide)
+    d_text_all = jnp.concatenate(strip_gather(d_text.reshape(2 * wide, texts)), axis=1)
+    text_sum = contract(states, d_text_all, 0, 1).astype(b16)
+    text_blocks = text_sum.reshape(PLANE, states_wide // PLANE, 2 * wide)
+    text_blocks = absolute(exchange(text_blocks, place, FLIP_PLACE), place)
+    text_key_grad = sheet(text_blocks, 0, wide)
+    text_value_grad = sheet(text_blocks, wide, wide)
+
+    vectors = strip_gather(plane_sum(jnp.stack([u_ffn, w_ffn, w_attn])))
+    last = strip_gather(plane_sum(u_attn))
+    items = []
+    for mask in range(4):
+        low_part = jnp.concatenate([attn_gain * last[mask], vectors[mask][2]])
+        high_part = jnp.concatenate([ffn_gain * vectors[mask][0], vectors[mask][1]])
+        items.append(jnp.where(first_core, low_part, high_part))
+    ada_bias_grad = pair_sum(items)
+    attn_gain_grad = pair_sum([last[m] * (1.0 + scale_attn_items[m]) for m in range(4)])
+    ffn_gain_grad = pair_sum([vectors[m][0] * (1.0 + scale_ffn_items[m]) for m in range(4)])
+    ada_rows = silu_embed.shape[1] // (STRIPS * PLANE)
+    silu_own = lax.dynamic_slice_in_dim(
+        silu_embed, (strip * PLANE + place) * ada_rows, ada_rows, 1
+    )
+    ada_grad = pair_sum(
+        [
+            lax.dynamic_index_in_dim(silu_own, item_band[strip ^ m], 0, keepdims=False)[:, None]
+            * items[m][None, :]
+            for m in range(4)
+        ]
+    )
+    head_parts = jnp.stack(
+        [gains[:, 0], gains[:, 128], gains[:, 256], gains[:, 384]]
+    )
+    head_parts = pair_sum(strip_gather(head_parts))
+    head_parts = absolute(
+        [head_parts] + [move(head_parts, FLIP_PLACE[m]) for m in (1, 2, 3)], place
+    )
+    head_parts = jnp.concatenate(head_parts, axis=1)
+    return (
+        block_out,
+        tokens_grad,
+        text_grad,
+        ada_grad,
+        ada_bias_grad,
+        attn_gain_grad,
+        ffn_gain_grad,
+        query_grad,
+        key_grad,
+        value_grad,
+        head_parts[0],
+        head_parts[1],
+        head_parts[3].reshape(-1, HDIM)[:, 0],
+        text_key_grad,
+        text_value_grad,
+        head_parts[2],
+        out_grad,
+        gate_grad,
+        up_grad,
+        down_grad,
+    )
+
+
+def placements(seq, tp):
+    ins = (
+        P(seq, None),
+        P(seq, None),
         P(),
         P(),
         P(),
         P(),
-        P("seq", None),
-        P(None, "tp"),
-        P("tp"),
+        P(seq, None),
+        P(None, tp),
+        P(tp),
         P(),
         P(),
-        P(None, "tp"),
-        P(None, "tp"),
-        P(None, "tp"),
-        P("tp"),
-        P("tp"),
-        P("tp"),
-        P(None, "tp"),
-        P(None, "tp"),
-        P("tp"),
-        P("tp", None),
-        P(None, "tp"),
-        P(None, "tp"),
-        P("tp", None),
-    )
-    return jax.shard_map(
-        shards,
-        mesh=mesh,
-        in_specs=placed,
-        out_specs=(
-            P("seq", None),
-            P("seq", None),
-            P("seq", "tp"),
-            P("seq", "tp"),
-            P("tp"),
-            P(),
-            P(),
-            P("seq", "tp"),
-            P("seq", "tp"),
-            P("seq", "tp"),
-            P("tp"),
-            P("tp"),
-            P("tp"),
-            P("seq", "tp"),
-            P("seq", "tp"),
-            P("tp"),
-            P("tp", "seq"),
-            P("seq", "tp"),
-            P("seq", "tp"),
-            P("tp", "seq"),
-        ),
-        check_vma=False,
-    )
+        P(None, tp),
+        P(None, tp),
+        P(None, tp),
+        P(tp),
+        P(tp),
+        P(tp),
+        P(None, tp),
+        P(None, tp),
+        P(tp),
+        P(tp, None),
+        P(None, tp),
+        P(None, tp),
+        P(tp, None),
+    )
+    outs = (
+        P(seq, None),
+        P(seq, None),
+        P(seq, tp),
+        P(seq, tp),
+        P(tp),
+        P(),
+        P(),
+        P(seq, tp),
+        P(seq, tp),
+        P(seq, tp),
+        P(tp),
+        P(tp),
+        P(tp),
+        P(seq, tp),
+        P(seq, tp),
+        P(tp),
+        P(tp, seq),
+        P(seq, tp),
+        P(seq, tp),
+        P(tp, seq),
+    )
+    return ins, outs
+
+
+def solution(mesh):
+    if mesh.shape["seq"] == STRIPS * PLANE and mesh.shape["tp"] == CORES:
+        body, seq, tp = strip_shards, ("z", "y", "x"), "c"
+        mesh = Mesh(mesh.devices.reshape(STRIPS, 2, 2, CORES), MESH_AXES)
+    else:
+        body, seq, tp = shards, "seq", "tp"
+    ins, outs = placements(seq, tp)
+    return jax.shard_map(body, mesh=mesh, in_specs=ins, out_specs=outs, check_vma=False)

time: 2770 us -> 530 us (0.19)
  the two profiles are of different devices: /device:TPU:0 before, /device:TPU:9 now
where the time goes in v1:
time: 530 us; the launch traced here: 519 us
  waiting for transfers between devices  183 us (35%)
  starting transfers between devices  84.2 us (16%)
  local copies, waits for them, and re-layouts  82.8 us (16%)
  matrix products  69.3 us (13%)
  other arithmetic  50.1 us (9%)
  between operations  26.3 us (5%)
  Pallas kernels  23.6 us (4%)
    ppermute x82, waiting for transfers between devices, move(): return lax.ppermute(value, MESH_AXES, pairs)  164 us
    ppermute x82, starting transfers between devices, move(): return lax.ppermute(value, MESH_AXES, pairs)  84.1 us
    dot_general x14, matrix products, contract(): lax.dot_general(left, right, (((left_dim,), (right_dim,)), ((), ())), pre...  52.2 us
    unnamed x282, local copies, waits for them, and re-layouts  36.5 us
    reduce_scatter x2, waiting for transfers between devices, spread(): own = lax.psum_scatter(grad, 'z', scatter_dimension=0, tiled=True)  18.6 us
    pallas_call x1, Pallas kernels, strip_shards(): attention_call(heads, lanes, texts, True)(*common, *saved, d_comb)  13.5 us
  transfers between devices with their start and end apart: 84, of which 38 were waited for; matrix products, arithmetic and copies ran while one was open for 30% of the time, Pallas kernels for 3%

profile of v1, /device:TPU:9, one launch (start us, length us, event | category | flops | bytes accessed | tf_op | source)
XLA Modules:
  0.0 519.0 jit_solution(11420394921444765445)
XLA Ops:
  23.5 5.3 %fusion.144 = f32[768,64]{1,0:T(8,128)S(1)} fusion(bf16[64,4096]{1,0:T(8,128)(2,1)S(1)} %copy-done.32, bf16[4096,768]{1,0:T(8,128)(2,1)} %param.41), kind=kOutput, calls=%fused_computation.479 | convolution fusion | flops 402653184 | bytes 7012352 | tf_op jit(solution)/shard_map/stack | solution.py:863
  45.5 5.3 %collective-permute-done.4 = bf16[128,1536]{1,0:T(8,128)(2,1)S(1)} collective-permute-done((bf16[128,1536]{1,0:T(8,128)(2,1)S(1)}, bf16[128,1536]{1,0:T(8,128)(2,1)S(1)}, u32[]{:S(2)}, u32[]{:S(2)}) %collective-permute-start.4) | collective-permute-done | bytes 393248 | tf_op jit(solution)/shard_map/ppermute | solution.py:493
  88.4 6.1 %fusion.11.q_ref.k_ref.v_ref = f32[576,1024]{1,0:T(8,128)} fusion(bf16[1024,1536]{1,0:T(8,128)(2,1)} %constant_dynamic-update-slice_fusion.11, f32[1536]{0:T(1024)S(1)} %mul.479, f32[1024]{0:T(1024)S(1)} %add_rsqrt_fusion, bf16[1536,192]{1,0:T(8,128)(2,1)S(1)} %copy-done.65, bf16[1536,192]{1,0:T(8,128)(2,1)S(1)} %copy-done.67, ...), kind=kOutput, calls=%fused_computation.62 | convolution fusion | flops 1823539200 | bytes 7284736 | tf_op jit(solution)/shard_map/dot_general | solution.py:539
  94.6 10.1 %shard_map.383 = (bf16[192,1024]{1,0:T(8,128)(2,1)S(1)}, f32[192,1024]{1,0:T(8,128)S(1)}, f32[192,1024]{1,0:T(8,128)S(1)}, bf16[192,1024]{1,0:T(8,128)(2,1)S(1)}...) custom-call(f32[576,1024]{1,0:T(8,128)} %fusion.11.q_ref.k_ref.v_ref, ...), custom_call_target="tpu_custom_call" | custom-call | flops 4026531840 | bytes 1572864 | tf_op jit(solution)/shard_map/pallas_call | solution.py:918
  117.4 5.3 %collective-permute-done.25 = bf16[32,1536]{1,0:T(8,128)(2,1)S(1)} collective-permute-done((bf16[32,1536]{1,0:T(8,128)(2,1)S(1)}, bf16[32,1536]{1,0:T(8,128)(2,1)S(1)}, u32[]{:S(2)}, u32[]{:S(2)}) %collective-permute-start.25) | collective-permute-done | bytes 98336 | tf_op jit(solution)/shard_map/ppermute | solution.py:493
  126.0 7.8 %collective-permute-done.12 = bf16[128,1536]{1,0:T(8,128)(2,1)S(1)} collective-permute-done((bf16[128,1536]{1,0:T(8,128)(2,1)S(1)}, bf16[128,1536]{1,0:T(8,128)(2,1)S(1)}, u32[]{:S(2)}, u32[]{:S(2)}) %collective-permute-start.12) | collective-permute-done | bytes 393248 | tf_op jit(solution)/shard_map/ppermute | solution.py:493
  144.2 9.1 %collective-permute-done.27 = bf16[256,1536]{1,0:T(8,128)(2,1)S(1)} collective-permute-done((bf16[256,1536]{1,0:T(8,128)(2,1)S(1)}, bf16[256,1536]{1,0:T(8,128)(2,1)S(1)}, u32[]{:S(2)}, u32[]{:S(2)}) %collective-permute-start.27) | collective-permute-done | bytes 786464 | tf_op jit(solution)/shard_map/ppermute | solution.py:493
  154.3 7.1 %collective-permute-done.14 = bf16[256,1536]{1,0:T(8,128)(2,1)S(1)} collective-permute-done((bf16[256,1536]{1,0:T(8,128)(2,1)S(1)}, bf16[256,1536]{1,0:T(8,128)(2,1)S(1)}, u32[]{:S(2)}, u32[]{:S(2)}) %collective-permute-start.14) | collective-permute-done | bytes 786464 | tf_op jit(solution)/shard_map/ppermute | solution.py:493
  168.5 6.2 %fusion.4 = f32[1024,1024]{0,1:T(8,128)S(1)} fusion(bf16[1536,512]{1,0:T(8,128)(2,1)S(1)} %get-tuple-element.266, bf16[1536,512]{1,0:T(8,128)(2,1)S(1)} %get-tuple-element.267, bf16[512,1536]{1,0:T(8,128)(2,1)} %collective-permute-done.15, bf16[256,1536]{1,0:T(8,128)(2,1)S(1)} %copy-done.61, bf16[128,1536]{1,0:T(8,128)(2,1)S(1)} %copy-done.44, ...), kind=kOutput, calls=%fused_computation.30 | convolution fusion | flops 3240099840 | bytes 10485760 | tf_op jit(solution)/shard_map/dot_general | solution.py:936
  197.4 5.4 %collective-permute-done.68 = bf16[64,1024]{1,0:T(8,128)(2,1)S(1)} collective-permute-done((bf16[64,1024]{1,0:T(8,128)(2,1)}, bf16[64,1024]{1,0:T(8,128)(2,1)S(1)}, u32[]{:S(2)}, u32[]{:S(2)}) %collective-permute-start.68) | collective-permute-done | bytes 131104 | tf_op jit(solution)/shard_map/ppermute | solution.py:493
  221.3 11.3 %collective-permute-done.72 = bf16[4,64,1024]{2,1,0:T(8,128)(2,1)S(1)} collective-permute-done((bf16[4,64,1024]{2,1,0:T(8,128)(2,1)S(1)}, bf16[4,64,1024]{2,1,0:T(8,128)(2,1)S(1)}, u32[]{:S(2)}, u32[]{:S(2)}) %collective-permute-start.72) | collective-permute-done | bytes 524320 | tf_op jit(solution)/shard_map/ppermute | solution.py:493
  234.4 7.2 %collective-permute-done.30 = bf16[256,1536]{1,0:T(8,128)(2,1)S(1)} collective-permute-done((bf16[256,1536]{1,0:T(8,128)(2,1)S(1)}, bf16[256,1536]{1,0:T(8,128)(2,1)S(1)}, u32[]{:S(2)}, u32[]{:S(2)}) %collective-permute-start.30) | collective-permute-done | bytes 786464 | tf_op jit(solution)/shard_map/ppermute | solution.py:493
  243.3 9.8 %collective-permute-done.17 = bf16[256,1536]{1,0:T(8,128)(2,1)S(1)} collective-permute-done((bf16[256,1536]{1,0:T(8,128)(2,1)S(1)}, bf16[256,1536]{1,0:T(8,128)(2,1)S(1)}, u32[]{:S(2)}, u32[]{:S(2)}) %collective-permute-start.17) | collective-permute-done | bytes 786464 | tf_op jit(solution)/shard_map/ppermute | solution.py:493
  255.2 6.5 %convolution_convert_fusion.3 = bf16[1536,1024]{0,1:T(8,128)(2,1)} fusion(bf16[1024,512]{0,1:T(8,128)(2,1)S(1)} %copy-done.128, bf16[1024,512]{0,1:T(8,128)(2,1)S(1)} %copy-done.126, bf16[512,1536]{1,0:T(8,128)(2,1)} %collective-permute-done.15, bf16[256,1536]{1,0:T(8,128)(2,1)S(1)} %copy-done.62, bf16[128,1536]{1,0:T(8,128)(2,1)S(1)} %copy-done.45, ...), kind=kOutput, calls=%fused_computation.11 | convolution fusion | flops 3239575552 | bytes 8388608 | tf_op jit(solution)/shard_map/dot_general | solution.py:539
  276.9 6.8 %collective-permute-done.33 = bf16[256,1536]{1,0:T(8,128)(2,1)S(1)} collective-permute-done((bf16[256,1536]{1,0:T(8,128)(2,1)S(1)}, bf16[256,1536]{1,0:T(8,128)(2,1)S(1)}, u32[]{:S(2)}, u32[]{:S(2)}) %collective-permute-start.33) | collective-permute-done | bytes 786464 | tf_op jit(solution)/shard_map/ppermute | solution.py:493
  301.5 13.5 %shard_map.384 = (bf16[192,1024]{1,0:T(8,128)(2,1)S(1)}, bf16[192,1024]{1,0:T(8,128)(2,1)S(1)}, bf16[192,1024]{1,0:T(8,128)(2,1)S(1)}, bf16[192,256]{1,0:T(8,128...) custom-call(f32[576,1024]{1,0:T(8,128)} %fusion.11.q_ref.k_ref.v_ref, ...), custom_call_target="tpu_custom_call" | custom-call | flops 10066329600 | bytes 1572864 | tf_op jit(solution)/shard_map/pallas_call | solution.py:960
  361.3 8.2 %copy.91 = bf16[1536,1728]{1,0:T(8,128)(2,1)} copy(bf16[1536,1728]{0,1:T(8,128)(2,1)} %pad_maximum_fusion) | data formatting | bytes 10616832
  386.2 5.5 %convolution_add_fusion = f32[64,4096]{1,0:T(8,128)S(1)} fusion(f32[64,4096]{1,0:T(8,128)S(1)} %fusion.36, bf16[4096,768]{1,0:T(8,128)(2,1)} %param.42, bf16[2,768,64]{2,1,0:T(8,128)(2,1)S(1)} %pad_maximum_fusion.29), kind=kOutput, calls=%fused_computation.7 | convolution fusion | flops 402915328 | bytes 8585216 | tf_op jit(solution)/shard_map/dot_general | solution.py:539
  407.2 8.3 %collective-permute-done.36 = bf16[256,1536]{1,0:T(8,128)(2,1)S(1)} collective-permute-done((bf16[256,1536]{1,0:T(8,128)(2,1)S(1)}, bf16[256,1536]{1,0:T(8,128)(2,1)S(1)}, u32[]{:S(2)}, u32[]{:S(2)}) %collective-permute-start.36) | collective-permute-done | bytes 786464 | tf_op jit(solution)/shard_map/ppermute | solution.py:493
  417.4 5.5 %collective-permute-done.37 = bf16[128,1536]{1,0:T(8,128)(2,1)S(1)} collective-permute-done((bf16[128,1536]{1,0:T(8,128)(2,1)S(1)}, bf16[128,1536]{1,0:T(8,128)(2,1)S(1)}, u32[]{:S(2)}, u32[]{:S(2)}) %collective-permute-start.37) | collective-permute-done | bytes 393248 | tf_op jit(solution)/shard_map/ppermute | solution.py:493
  440.5 9.5 %collective-permute-done.38 = bf16[32,1536]{1,0:T(8,128)(2,1)S(1)} collective-permute-done((bf16[32,1536]{1,0:T(8,128)(2,1)S(1)}, bf16[32,1536]{1,0:T(8,128)(2,1)S(1)}, u32[]{:S(2)}, u32[]{:S(2)}) %collective-permute-start.38) | collective-permute-done | bytes 98336 | tf_op jit(solution)/shard_map/ppermute | solution.py:493
  450.0 5.3 %collective-permute-done.39 = bf16[32,1536]{1,0:T(8,128)(2,1)S(1)} collective-permute-done((bf16[32,1536]{1,0:T(8,128)(2,1)S(1)}, bf16[32,1536]{1,0:T(8,128)(2,1)S(1)}, u32[]{:S(2)}, u32[]{:S(2)}) %collective-permute-start.39) | collective-permute-done | bytes 98336 | tf_op jit(solution)/shard_map/ppermute | solution.py:493
  468.7 18.6 %reduce-scatter.9.cloned.1.call-done = bf16[384,1728]{1,0:T(8,128)(2,1)} async-done(((bf16[1536,1728]{1,0:T(8,128)(2,1)}), bf16[384,1728]{1,0:T(8,128)(2,1)}) %reduce-scatter.9.cloned.1.call-update) | async-done | bytes 1327120 | tf_op jit(solution)/shard_map/reduce_scatter | solution.py:976
  498.7 8.2 %collective-permute-done.80 = bf16[96,1728]{1,0:T(8,128)(2,1)S(1)} collective-permute-done((bf16[96,1728]{1,0:T(8,128)(2,1)S(1)}, bf16[96,1728]{1,0:T(8,128)(2,1)S(1)}, u32[]{:S(2)}, u32[]{:S(2)}) %collective-permute-start.80) | collective-permute-done | bytes 331808 | tf_op jit(solution)/shard_map/ppermute | solution.py:493
  (611 shorter events, 300.8 us)
Async XLA Ops:
  7.2 450.1 %reduce-scatter.7.cloned.1.call-start = ((), (), s32[]{:S(2)}) async-start(), calls=%async_computation.2 | async-start | bytes 2457600 | tf_op jit(solution)/shard_map/reduce_scatter | solution.py:976
  9.2 26.3 %collective-permute-start = (bf16[32,1536]{1,0:T(8,128)(2,1)}, bf16[32,1536]{1,0:T(8,128)(2,1)}, u32[]{:S(2)}, u32[]{:S(2)}) collective-permute-start(bf16[32,1536]{1,0:T(8,128)(2,1)} %get-tuple-element.141), channel_id=1, source_target_pairs={{0,8},{1,9},{2,10},{3,11},{4,12},{5,13},{6,14},{7,15},{8,0},{9,1},... | collective-permute-start | bytes 294920 | tf_op jit(solution)/shard_map/ppermute | solution.py:493
  9.2 27.6 %collective-permute-start.1 = (bf16[32,1536]{1,0:T(8,128)(2,1)}, bf16[32,1536]{1,0:T(8,128)(2,1)}, u32[]{:S(2)}, u32[]{:S(2)}) collective-permute-start(bf16[32,1536]{1,0:T(8,128)(2,1)} %get-tuple-element.140), channel_id=1, source_target_pairs={{0,16},{1,17},{2,18},{3,19},{4,20},{5,21},{6,22},{7,23},{8,24},{9,... | collective-permute-start | bytes 294920 | tf_op jit(solution)/shard_map/ppermute | solution.py:493
  11.7 25.3 %collective-permute-start.2 = (bf16[32,1536]{1,0:T(8,128)(2,1)}, bf16[32,1536]{1,0:T(8,128)(2,1)}, u32[]{:S(2)}, u32[]{:S(2)}) collective-permute-start(bf16[32,1536]{1,0:T(8,128)(2,1)} %get-tuple-element.139), channel_id=1, source_target_pairs={{0,24},{1,25},{2,26},{3,27},{4,28},{5,29},{6,30},{7,31},{8,16},{9,... | collective-permute-start | bytes 294920 | tf_op jit(solution)/shard_map/ppermute | solution.py:493
  17.0 62.4 %collective-permute-start.3 = (f32[4,3072]{1,0:T(4,128)}, f32[4,3072]{1,0:T(4,128)}, u32[]{:S(2)}, u32[]{:S(2)}) collective-permute-start(f32[4,3072]{1,0:T(4,128)} %fusion.43), channel_id=1, source_target_pairs={{0,1},{1,0},{2,3},{3,2},{4,5},{5,4},{6,7},{7,6},{8,9},{9,8},{10,11... | collective-permute-start | bytes 147464 | tf_op jit(solution)/shard_map/ppermute | solution.py:493
  30.7 50.8 %collective-permute-start.7 = (f32[2,192,64]{2,1,0:T(8,128)}, f32[2,192,64]{2,1,0:T(8,128)}, u32[]{:S(2)}, u32[]{:S(2)}) collective-permute-start(f32[2,192,64]{2,1,0:T(8,128)} %get-tuple-element.134), channel_id=1, source_target_pairs={{0,2},{1,3},{2,0},{3,1},{4,6},{5,7},{6,4},{7,5},{8,10},{9,11},{10,... | collective-permute-start | bytes 294920 | tf_op jit(solution)/shard_map/ppermute | solution.py:493
  35.4 46.1 %collective-permute-start.8 = (f32[2,192,64]{2,1,0:T(8,128)}, f32[2,192,64]{2,1,0:T(8,128)}, u32[]{:S(2)}, u32[]{:S(2)}) collective-permute-start(f32[2,192,64]{2,1,0:T(8,128)} %get-tuple-element.135), channel_id=1, source_target_pairs={{0,4},{1,5},{2,6},{3,7},{4,0},{5,1},{6,2},{7,3},{8,12},{9,13},{10,... | collective-permute-start | bytes 294920 | tf_op jit(solution)/shard_map/ppermute | solution.py:493
  36.8 44.8 %collective-permute-start.9 = (f32[2,192,64]{2,1,0:T(8,128)}, f32[2,192,64]{2,1,0:T(8,128)}, u32[]{:S(2)}, u32[]{:S(2)}) collective-permute-start(f32[2,192,64]{2,1,0:T(8,128)} %get-tuple-element.136), channel_id=1, source_target_pairs={{0,6},{1,7},{2,4},{3,5},{4,2},{5,3},{6,0},{7,1},{8,14},{9,15},{10,... | collective-permute-start | bytes 294920 | tf_op jit(solution)/shard_map/ppermute | solution.py:493
  141.8 19.6 %collective-permute-start.14 = (bf16[256,1536]{1,0:T(8,128)(2,1)S(1)}, bf16[256,1536]{1,0:T(8,128)(2,1)S(1)}, u32[]{:S(2)}, u32[]{:S(2)}) collective-permute-start(bf16[256,1536]{1,0:T(8,128)(2,1)S(1)} %pad_maximum_fusion.13), channel_id=1, source_target_pairs={{0,4},{1,3},{2,6},{3,1},{4,0},{5,7},{6,2},{7,5},{8,12},{9,11},{10,... | collective-permute-start | bytes 2359304 | tf_op jit(solution)/shard_map/ppermute | solution.py:493
  183.0 27.7 %collective-permute-start.29 = (bf16[512,1536]{1,0:T(8,128)(2,1)}, bf16[512,1536]{1,0:T(8,128)(2,1)}, u32[]{:S(2)}, u32[]{:S(2)}) collective-permute-start(bf16[512,1536]{1,0:T(8,128)(2,1)} %slice.468), channel_id=1, source_target_pairs={{0,1},{1,0},{2,3},{3,2},{4,5},{5,4},{6,7},{7,6},{8,9},{9,8},{10,11... | collective-permute-start | bytes 4718600 | tf_op jit(solution)/shard_map/ppermute | solution.py:493
  187.6 26.7 %collective-permute-start.16 = (bf16[512,1536]{1,0:T(8,128)(2,1)}, bf16[512,1536]{1,0:T(8,128)(2,1)}, u32[]{:S(2)}, u32[]{:S(2)}) collective-permute-start(bf16[512,1536]{1,0:T(8,128)(2,1)} %slice.458), channel_id=1, source_target_pairs={{0,1},{1,0},{2,3},{3,2},{4,5},{5,4},{6,7},{7,6},{8,9},{9,8},{10,11... | collective-permute-start | bytes 4718600 | tf_op jit(solution)/shard_map/ppermute | solution.py:493
  210.7 21.9 %collective-permute-start.72 = (bf16[4,64,1024]{2,1,0:T(8,128)(2,1)S(1)}, bf16[4,64,1024]{2,1,0:T(8,128)(2,1)S(1)}, u32[]{:S(2)}, u32[]{:S(2)}) collective-permute-start(bf16[4,64,1024]{2,1,0:T(8,128)(2,1)S(1)} %get-tuple-element.151), channel_id=1, source_target_pairs={{0,6},{1,7},{2,4},{3,5},{4,2},{5,3},{6,0},{7,1},{8,14},{9,15},{10,... | collective-permute-start | bytes 1572872 | tf_op jit(solution)/shard_map/ppermute | solution.py:493
  213.1 28.5 %collective-permute-start.30 = (bf16[256,1536]{1,0:T(8,128)(2,1)S(1)}, bf16[256,1536]{1,0:T(8,128)(2,1)S(1)}, u32[]{:S(2)}, u32[]{:S(2)}) collective-permute-start(bf16[256,1536]{1,0:T(8,128)(2,1)S(1)} %slice.672), channel_id=1, source_target_pairs={{0,4},{1,3},{2,6},{3,1},{4,0},{5,7},{6,2},{7,5},{8,12},{9,11},{10,... | collective-permute-start | bytes 2359304 | tf_op jit(solution)/shard_map/ppermute | solution.py:493
  216.3 36.9 %collective-permute-start.17 = (bf16[256,1536]{1,0:T(8,128)(2,1)S(1)}, bf16[256,1536]{1,0:T(8,128)(2,1)S(1)}, u32[]{:S(2)}, u32[]{:S(2)}) collective-permute-start(bf16[256,1536]{1,0:T(8,128)(2,1)S(1)} %slice.673), channel_id=1, source_target_pairs={{0,4},{1,3},{2,6},{3,1},{4,0},{5,7},{6,2},{7,5},{8,12},{9,11},{10,... | collective-permute-start | bytes 2359304 | tf_op jit(solution)/shard_map/ppermute | solution.py:493
  241.9 19.9 %collective-permute-start.31 = (bf16[128,1536]{1,0:T(8,128)(2,1)S(1)}, bf16[128,1536]{1,0:T(8,128)(2,1)S(1)}, u32[]{:S(2)}, u32[]{:S(2)}) collective-permute-start(bf16[128,1536]{1,0:T(8,128)(2,1)S(1)} %slice.676), channel_id=1, source_target_pairs={{0,2},{1,5},{2,0},{3,7},{4,6},{5,1},{6,4},{7,3},{8,10},{9,13},{10,... | collective-permute-start | bytes 1179656 | tf_op jit(solution)/shard_map/ppermute | solution.py:493
  296.7 31.7 %collective-permute-start.55 = (f32[3,1536]{1,0:T(4,128)S(1)}, f32[3,1536]{1,0:T(4,128)}, u32[]{:S(2)}, u32[]{:S(2)}) collective-permute-start(f32[3,1536]{1,0:T(4,128)S(1)} %add.636), channel_id=1, source_target_pairs={{0,16},{1,17},{2,18},{3,19},{4,20},{5,21},{6,22},{7,23},{8,24},{9,... | collective-permute-start | bytes 55304 | tf_op jit(solution)/shard_map/ppermute | solution.py:493
  297.3 32.6 %collective-permute-start.57 = (f32[3,1536]{1,0:T(4,128)S(1)}, f32[3,1536]{1,0:T(4,128)}, u32[]{:S(2)}, u32[]{:S(2)}) collective-permute-start(f32[3,1536]{1,0:T(4,128)S(1)} %add.636), channel_id=1, source_target_pairs={{0,24},{1,25},{2,26},{3,27},{4,28},{5,29},{6,30},{7,31},{8,16},{9,... | collective-permute-start | bytes 55304 | tf_op jit(solution)/shard_map/ppermute | solution.py:493
  325.3 161.9 %reduce-scatter.9.cloned.1.call-start = ((), (), s32[]{:S(2)}) async-start(), calls=%async_computation.3 | async-start | bytes 6881280 | tf_op jit(solution)/shard_map/reduce_scatter | solution.py:976
  335.4 56.7 %collective-permute-start.73 = (bf16[384,256]{1,0:T(8,128)(2,1)}, bf16[384,256]{1,0:T(8,128)(2,1)}, u32[]{:S(2)}, u32[]{:S(2)}) collective-permute-start(bf16[384,256]{1,0:T(8,128)(2,1)} %bitcast.59), channel_id=1, source_target_pairs={{0,8},{1,9},{2,10},{3,11},{4,12},{5,13},{6,14},{7,15},{8,0},{9,1},... | collective-permute-start | bytes 589832 | tf_op jit(solution)/shard_map/ppermute | solution.py:493
  338.0 54.1 %collective-permute-start.74 = (bf16[384,256]{1,0:T(8,128)(2,1)}, bf16[384,256]{1,0:T(8,128)(2,1)}, u32[]{:S(2)}, u32[]{:S(2)}) collective-permute-start(bf16[384,256]{1,0:T(8,128)(2,1)} %bitcast.59), channel_id=1, source_target_pairs={{0,16},{1,17},{2,18},{3,19},{4,20},{5,21},{6,22},{7,23},{8,24},{9,... | collective-permute-start | bytes 589832 | tf_op jit(solution)/shard_map/ppermute | solution.py:493
  340.8 17.6 %collective-permute-start.63 = (f32[4,192]{1,0:T(4,128)S(1)}, f32[4,192]{1,0:T(4,128)S(1)}, u32[]{:S(2)}, u32[]{:S(2)}) collective-permute-start(f32[4,192]{1,0:T(4,128)S(1)} %pad_maximum_fusion.34), channel_id=1, source_target_pairs={{0,24},{1,25},{2,26},{3,27},{4,28},{5,29},{6,30},{7,31},{8,16},{9,... | collective-permute-start | bytes 9224 | tf_op jit(solution)/shard_map/ppermute | solution.py:493
  378.6 18.9 %collective-permute-start.35 = (bf16[512,1536]{1,0:T(8,128)(2,1)}, bf16[512,1536]{1,0:T(8,128)(2,1)S(1)}, u32[]{:S(2)}, u32[]{:S(2)}) collective-permute-start(bf16[512,1536]{1,0:T(8,128)(2,1)} %slice.474), channel_id=1, source_target_pairs={{0,1},{1,0},{2,3},{3,2},{4,5},{5,4},{6,7},{7,6},{8,9},{9,8},{10,11... | collective-permute-start | bytes 4718600 | tf_op jit(solution)/shard_map/ppermute | solution.py:493
  398.0 17.5 %collective-permute-start.36 = (bf16[256,1536]{1,0:T(8,128)(2,1)S(1)}, bf16[256,1536]{1,0:T(8,128)(2,1)S(1)}, u32[]{:S(2)}, u32[]{:S(2)}) collective-permute-start(bf16[256,1536]{1,0:T(8,128)(2,1)S(1)} %slice.671), channel_id=1, source_target_pairs={{0,4},{1,3},{2,6},{3,1},{4,0},{5,7},{6,2},{7,5},{8,12},{9,11},{10,... | collective-permute-start | bytes 2359304 | tf_op jit(solution)/shard_map/ppermute | solution.py:493
  435.1 20.2 %collective-permute-start.39 = (bf16[32,1536]{1,0:T(8,128)(2,1)S(1)}, bf16[32,1536]{1,0:T(8,128)(2,1)S(1)}, u32[]{:S(2)}, u32[]{:S(2)}) collective-permute-start(bf16[32,1536]{1,0:T(8,128)(2,1)S(1)} %get-tuple-element.163), channel_id=1, source_target_pairs={{0,16},{1,17},{2,18},{3,19},{4,20},{5,21},{6,22},{7,23},{8,24},{9,... | collective-permute-start | bytes 294920 | tf_op jit(solution)/shard_map/ppermute | solution.py:493
  (191 other events, 2106.6 us)
Sparse Core Ops, SparseCore 0:
  325.5 52.0 reduce-scatter.6
  379.8 107.3 reduce-scatter.8
